TPU v7x, 256 devices: a whole 4x4x8 slice. The times are simulated.
256 devices in a mesh: ctx: 32 (over x_lo, z, core), head: 8 (over y, x_hi).
Axes of the slice: x: 4 (x_hi: 2, x_lo: 2; x = x_hi * 2 + x_lo), y: 4, z: 8, core: 2. Of those that a mesh axis runs over, the one named last changes fastest.
Arguments:
- query_latent: bfloat16 [4096, 128, 512], P('ctx', 'head'), may hold values from -64 to 64
- query_rope: bfloat16 [4096, 8192], P('ctx', 'head'), may hold values from -3 to 3
- latent: bfloat16 [4096, 512], P('ctx'), may hold values from -4 to 4
- rope_key: bfloat16 [64, 4096], P(None, 'ctx'), may hold values from -5 to 5
- out_grad: bfloat16 [4096, 128, 512], P('ctx', 'head'), may hold values from -0.59765625 to 0.59765625
- doc_lengths: int32 [16], replicated, may hold values from 1 to 512, 4096 in all
Outputs:
- query_grad: bfloat16 [4096, 128, 512], P('ctx', 'head')
- query_rope_grad: bfloat16 [4096, 8192], P('ctx', 'head')
- latent_grad: bfloat16 [4096, 512], P('ctx')
- rope_key_grad: bfloat16 [64, 4096], P(None, 'ctx')
Inputs may be any that keep to these rules, and one draw needn't show every extreme that they name: `doc_lengths`: the lengths sum to 4096; the longest document is exactly 512 positions long.
All inputs are finite; a program needn't handle non-finite values.
Results may differ from a plain program's by a relative error of at most 0.0083.
Values may be sent and summed in bfloat16 or wider, within the bound.
A program may use at most 64 MiB of HBM per device.

v0:
```python
import jax
import jax.numpy as jnp
from jax import lax
from jax.sharding import PartitionSpec as P

SPAN = 4


softmax_scale = 192.0 ** (-0.5)


def from_behind(shard, axis, by):
    count = lax.axis_size(axis)
    pairs = [(i, i + by) for i in range(count) if 0 <= i + by < count]
    return lax.ppermute(shard, axis, pairs)


def as_sent(shard):

    def short(part):
        return part.astype(jnp.bfloat16) if part.dtype == jnp.float32 else part

    return jax.tree.map(short, shard)


def doc_index(positions, doc_ends):
    return jnp.sum((positions[:, None] >= doc_ends[None, :]).astype(jnp.int32), axis=1)


def local(query_latent, query_rope, latent, rope_key, out_grad, doc_lengths):
    tok_rows = latent.shape[0]
    head_count = query_latent.shape[1]
    rope_dim = rope_key.shape[0]
    shard_index = lax.axis_index("ctx")
    doc_ends = jnp.cumsum(doc_lengths)
    offsets = jnp.arange(tok_rows, dtype=jnp.int32)
    fetched = [(latent, rope_key)]
    for distance in range(1, SPAN + 1):
        fetched.append(from_behind((latent, rope_key), "ctx", distance))
    key_lat = jnp.concatenate([pair[0] for pair in fetched], axis=0)
    key_rope = jnp.concatenate([pair[1] for pair in fetched], axis=1)
    key_pos = jnp.concatenate(
        [(shard_index - distance) * tok_rows + offsets for distance in range(SPAN + 1)]
    )
    query_pos = shard_index * tok_rows + offsets
    allowed = (key_pos[None, :] >= 0) & (key_pos[None, :] <= query_pos[:, None])
    allowed = allowed & (
        doc_index(key_pos, doc_ends)[None, :] == doc_index(query_pos, doc_ends)[:, None]
    )
    rope_queries = query_rope.reshape(tok_rows, head_count, rope_dim)
    scores = jnp.einsum("thc,kc->thk", query_latent, key_lat, preferred_element_type=jnp.float32)
    scores = scores + jnp.einsum(
        "thr,rk->thk", rope_queries, key_rope, preferred_element_type=jnp.float32
    )
    scores = jnp.where(allowed[:, None, :], scores * softmax_scale, -jnp.inf)
    row_max = jnp.max(scores, axis=-1, keepdims=True)
    weights_exp = jnp.exp(scores - row_max)
    probs = weights_exp / jnp.sum(weights_exp, axis=-1, keepdims=True)
    probs_b = probs.astype(jnp.bfloat16)
    attn_out = jnp.einsum("thk,kc->thc", probs_b, key_lat, preferred_element_type=jnp.float32)
    row_delta = jnp.sum(out_grad.astype(jnp.float32) * attn_out, axis=-1)
    prob_grad = jnp.einsum("thc,kc->thk", out_grad, key_lat, preferred_element_type=jnp.float32)
    score_grad = (probs * (prob_grad - row_delta[:, :, None]) * softmax_scale).astype(jnp.bfloat16)
    query_grad = jnp.einsum(
        "thk,kc->thc", score_grad, key_lat, preferred_element_type=jnp.float32
    ).astype(jnp.bfloat16)
    rope_grad = jnp.einsum("thk,rk->thr", score_grad, key_rope, preferred_element_type=jnp.float32)
    query_rope_grad = rope_grad.astype(jnp.bfloat16).reshape(tok_rows, head_count * rope_dim)
    lat_terms = jnp.einsum("thk,thc->kc", probs_b, out_grad, preferred_element_type=jnp.float32)
    lat_terms = lat_terms + jnp.einsum(
        "thk,thc->kc", score_grad, query_latent, preferred_element_type=jnp.float32
    )
    rope_terms = jnp.einsum(
        "thk,thr->rk", score_grad, rope_queries, preferred_element_type=jnp.float32
    )

    def block_terms(distance):
        return (
            lat_terms[distance * tok_rows : (distance + 1) * tok_rows],
            rope_terms[:, distance * tok_rows : (distance + 1) * tok_rows],
        )

    own_lat, own_rope = block_terms(0)
    total_lat, total_rope = (own_lat, own_rope)
    for distance in range(1, SPAN + 1):
        back_lat, back_rope = from_behind(as_sent(block_terms(distance)), "ctx", -distance)
        total_lat = total_lat + back_lat
        total_rope = total_rope + back_rope
    summed_lat, summed_rope = lax.psum((total_lat, total_rope), "head")
    return (
        query_grad,
        query_rope_grad,
        summed_lat.astype(jnp.bfloat16),
        summed_rope.astype(jnp.bfloat16),
    )


def solution(mesh):
    in_specs = (
        P("ctx", "head", None),
        P("ctx", "head"),
        P("ctx", None),
        P(None, "ctx"),
        P("ctx", "head", None),
        P(),
    )
    out_specs = (P("ctx", "head", None), P("ctx", "head"), P("ctx", None), P(None, "ctx"))
    return jax.shard_map(local, mesh=mesh, in_specs=in_specs, out_specs=out_specs, check_vma=False)
```

profile of v0, /device:TPU:2, one launch (start us, length us, event | category | flops | bytes accessed | tf_op | source)
XLA Modules:
  0.0 158.3 jit_solution(9322499126792970790)
XLA Ops:
  0.6 3.4 %collective-permute-start.6 = (bf16[64,128]{1,0:T(8,128)(2,1)}, bf16[64,128]{1,0:T(8,128)(2,1)S(1)}, u32[]{:S(2)}, u32[]{:S(2)}) collective-permute-start(bf16[64,128]{1,0:T(8,128)(2,1)} %param.9), channel_id=1, source_target_pairs={{0,24},{8,32},{16,40},{24,48},{32,56},{40,64},{48,72},{56,80},{64,... | collective-permute-start | bytes 49160 | tf_op jit(solution)/shard_map/ppermute | solution.py:15
  4.1 3.8 %collective-permute-start.5 = (bf16[64,128]{1,0:T(8,128)(2,1)}, bf16[64,128]{1,0:T(8,128)(2,1)S(1)}, u32[]{:S(2)}, u32[]{:S(2)}) collective-permute-start(bf16[64,128]{1,0:T(8,128)(2,1)} %param.9), channel_id=1, source_target_pairs={{0,16},{8,24},{16,32},{24,40},{32,48},{40,56},{48,64},{56,72},{64,... | collective-permute-start | bytes 49160 | tf_op jit(solution)/shard_map/ppermute | solution.py:15
  7.9 3.7 %collective-permute-start.4 = (bf16[64,128]{1,0:T(8,128)(2,1)}, bf16[64,128]{1,0:T(8,128)(2,1)S(1)}, u32[]{:S(2)}, u32[]{:S(2)}) collective-permute-start(bf16[64,128]{1,0:T(8,128)(2,1)} %param.9), channel_id=1, source_target_pairs={{0,8},{8,16},{16,24},{24,32},{32,40},{40,48},{48,56},{56,64},{64,7... | collective-permute-start | bytes 49160 | tf_op jit(solution)/shard_map/ppermute | solution.py:15
  11.6 5.5 %collective-permute-start.7 = (bf16[64,128]{1,0:T(8,128)(2,1)}, bf16[64,128]{1,0:T(8,128)(2,1)S(1)}, u32[]{:S(2)}, u32[]{:S(2)}) collective-permute-start(bf16[64,128]{1,0:T(8,128)(2,1)} %param.9), channel_id=1, source_target_pairs={{0,32},{8,40},{16,48},{24,56},{32,64},{40,72},{48,80},{56,88},{64,... | collective-permute-start | bytes 49160 | tf_op jit(solution)/shard_map/ppermute | solution.py:15
  17.1 2.5 %collective-permute-start.2 = (bf16[128,512]{1,0:T(8,128)(2,1)}, bf16[128,512]{1,0:T(8,128)(2,1)S(1)}, u32[]{:S(2)}, u32[]{:S(2)}) collective-permute-start(bf16[128,512]{1,0:T(8,128)(2,1)} %param.8), channel_id=1, source_target_pairs={{0,24},{8,32},{16,40},{24,48},{32,56},{40,64},{48,72},{56,80},{64,... | collective-permute-start | bytes 393224 | tf_op jit(solution)/shard_map/ppermute | solution.py:15
  22.8 1.1 copy.39
  23.9 2.9 %collective-permute-start.1 = (bf16[128,512]{1,0:T(8,128)(2,1)}, bf16[128,512]{1,0:T(8,128)(2,1)S(1)}, u32[]{:S(2)}, u32[]{:S(2)}) collective-permute-start(bf16[128,512]{1,0:T(8,128)(2,1)} %param.8), channel_id=1, source_target_pairs={{0,16},{8,24},{16,32},{24,40},{32,48},{40,56},{48,64},{56,72},{64,... | collective-permute-start | bytes 393224 | tf_op jit(solution)/shard_map/ppermute | solution.py:15
  26.9 1.9 %collective-permute-start = (bf16[128,512]{1,0:T(8,128)(2,1)}, bf16[128,512]{1,0:T(8,128)(2,1)S(1)}, u32[]{:S(2)}, u32[]{:S(2)}) collective-permute-start(bf16[128,512]{1,0:T(8,128)(2,1)} %param.8), channel_id=1, source_target_pairs={{0,8},{8,16},{16,24},{24,32},{32,40},{40,48},{48,56},{56,64},{64,7... | collective-permute-start | bytes 393224 | tf_op jit(solution)/shard_map/ppermute | solution.py:15
  28.8 2.2 %collective-permute-start.3 = (bf16[128,512]{1,0:T(8,128)(2,1)}, bf16[128,512]{1,0:T(8,128)(2,1)S(1)}, u32[]{:S(2)}, u32[]{:S(2)}) collective-permute-start(bf16[128,512]{1,0:T(8,128)(2,1)} %param.8), channel_id=1, source_target_pairs={{0,32},{8,40},{16,48},{24,56},{32,64},{40,72},{48,80},{56,88},{64,... | collective-permute-start | bytes 393224 | tf_op jit(solution)/shard_map/ppermute | solution.py:15
  31.1 3.2 %fusion.27 = f32[640,128,16]{1,0,2:T(8,128)} fusion(bf16[128,16,64]{0,2,1:T(8,128)(2,1)S(1)} %bitcast.49, bf16[64,640]{1,0:T(8,128)(2,1)S(1)} %constant_dynamic-update-slice_fusion.6), kind=kOutput, calls=%fused_computation.31 | convolution fusion | flops 167772160 | bytes 5586944 | tf_op jit(solution)/shard_map/thr,rk->thk/dot_general | solution.py:52
  34.3 1.7 %collective-permute-done = bf16[128,512]{1,0:T(8,128)(2,1)S(1)} collective-permute-done((bf16[128,512]{1,0:T(8,128)(2,1)}, bf16[128,512]{1,0:T(8,128)(2,1)S(1)}, u32[]{:S(2)}, u32[]{:S(2)}) %collective-permute-start) | collective-permute-done | bytes 131104 | tf_op jit(solution)/shard_map/ppermute | solution.py:15
  36.0 4.5 %collective-permute-done.3 = bf16[128,512]{1,0:T(8,128)(2,1)S(1)} collective-permute-done((bf16[128,512]{1,0:T(8,128)(2,1)}, bf16[128,512]{1,0:T(8,128)(2,1)S(1)}, u32[]{:S(2)}, u32[]{:S(2)}) %collective-permute-start.3) | collective-permute-done | bytes 131104 | tf_op jit(solution)/shard_map/ppermute | solution.py:15
  40.5 7.9 %fusion.34 = (f32[128,16]{0,1:T(8,128)S(1)}, f32[128,16,640]{0,2,1:T(8,128)}) fusion(f32[640,128,16]{1,0,2:T(8,128)} %fusion.27, pred[128,640]{0,1:T(8,128)(4,1)S(1)} %compare_and_fusion, bf16[128,16,512]{2,1,0:T(8,128)(2,1)S(1)} %copy-done, bf16[640,512]{1,0:T(8,128)(2,1)S(1)} %constant_dynamic-update-slice_fusion.1), kind=kOutput, calls=%fused_computation.58 | convolution fusion | flops 1348731520 | bytes 13328384 | tf_op jit(solution)/shard_map/sub | solution.py:57
  48.4 3.3 %fusion.3 = bf16[128,16,640]{0,2,1:T(8,128)(2,1)S(1)} fusion(f32[128,16,640]{0,2,1:T(8,128)} %get-tuple-element.27, f32[128,16]{0,1:T(8,128)S(1)} %get-tuple-element.26), kind=kLoop, calls=%fused_computation.8 | loop fusion | flops 2621440 | bytes 7872512 | tf_op jit(solution)/shard_map/convert_element_type | solution.py:59
  51.7 4.0 %multiply_reduce_fusion = f32[128,16]{0,1:T(8,128)S(1)} fusion(bf16[128,16,640]{0,2,1:T(8,128)(2,1)S(1)} %fusion.3, bf16[128,16,512]{2,1,0:T(8,128)(2,1)S(1)} %copy-done.1, bf16[640,512]{1,0:T(8,128)(2,1)S(1)} %constant_dynamic-update-slice_fusion.1), kind=kOutput, calls=%fused_computation.6 | convolution fusion | flops 1345320960 | bytes 5382144 | tf_op jit(solution)/shard_map/thk,kc->thc/dot_general | solution.py:60
  55.7 2.8 %fusion.10 = f32[640,512]{1,0:T(8,128)S(1)} fusion(bf16[128,16,640]{0,2,1:T(8,128)(2,1)S(1)} %fusion.3, bf16[128,16,512]{2,1,0:T(8,128)(2,1)S(1)} %copy-done.1), kind=kOutput, calls=%fused_computation.16 | convolution fusion | flops 1342177280 | bytes 6029312 | tf_op jit(solution)/shard_map/thk,thc->kc/dot_general | solution.py:69
  58.6 4.3 %fusion.2 = bf16[128,16,640]{0,2,1:T(8,128)(2,1)S(1)} fusion(f32[128,16]{0,1:T(8,128)S(1)} %multiply_reduce_fusion, f32[128,16,640]{0,2,1:T(8,128)S(1)} %bitcast.48, f32[128,16]{0,1:T(8,128)S(1)} %get-tuple-element.26, bf16[128,16,512]{2,1,0:T(8,128)(2,1)S(1)} %copy-done.1, bf16[640,512]{1,0:T(8,128)(2,1)S(1)} %constant_dynamic-update-slice_fusion.1), kind=kOutput, calls=%fused_computation.3 | convolution fusion | flops 1348730880 | bytes 10633216 | tf_op jit(solution)/shard_map/thc,kc->thk/dot_general | solution.py:62
  64.4 3.2 %convolution_convert_fusion = bf16[128,16,512]{2,0,1:T(8,128)(2,1)} fusion(bf16[128,16,640]{0,2,1:T(8,128)(2,1)S(1)} %fusion.2, bf16[640,512]{1,0:T(8,128)(2,1)S(1)} %constant_dynamic-update-slice_fusion.1), kind=kOutput, calls=%fused_computation.9 | convolution fusion | flops 1343225856 | bytes 5373952 | tf_op jit(solution)/shard_map/thk,kc->thc/dot_general | solution.py:64
  67.6 4.7 %collective-permute-start.12 = (bf16[64,128]{1,0:T(8,128)(2,1)S(1)}, bf16[64,128]{1,0:T(8,128)(2,1)S(1)}, u32[]{:S(2)}, u32[]{:S(2)}) collective-permute-start(bf16[64,128]{1,0:T(8,128)(2,1)S(1)} %get-tuple-element.22), channel_id=1, source_target_pairs={{8,0},{16,8},{24,16},{32,24},{40,32},{48,40},{56,48},{64,56},{72,6... | collective-permute-start | bytes 49160 | tf_op jit(solution)/shard_map/ppermute | solution.py:15
  72.3 3.5 %collective-permute-start.15 = (bf16[64,128]{1,0:T(8,128)(2,1)S(1)}, bf16[64,128]{1,0:T(8,128)(2,1)S(1)}, u32[]{:S(2)}, u32[]{:S(2)}) collective-permute-start(bf16[64,128]{1,0:T(8,128)(2,1)S(1)} %get-tuple-element.23), channel_id=1, source_target_pairs={{32,0},{40,8},{48,16},{56,24},{64,32},{72,40},{80,48},{88,56},{96,... | collective-permute-start | bytes 49160 | tf_op jit(solution)/shard_map/ppermute | solution.py:15
  75.8 4.3 %collective-permute-start.14 = (bf16[64,128]{1,0:T(8,128)(2,1)S(1)}, bf16[64,128]{1,0:T(8,128)(2,1)S(1)}, u32[]{:S(2)}, u32[]{:S(2)}) collective-permute-start(bf16[64,128]{1,0:T(8,128)(2,1)S(1)} %get-tuple-element.24), channel_id=1, source_target_pairs={{24,0},{32,8},{40,16},{48,24},{56,32},{64,40},{72,48},{80,56},{88,... | collective-permute-start | bytes 49160 | tf_op jit(solution)/shard_map/ppermute | solution.py:15
  80.1 2.0 %collective-permute-start.13 = (bf16[64,128]{1,0:T(8,128)(2,1)S(1)}, bf16[64,128]{1,0:T(8,128)(2,1)S(1)}, u32[]{:S(2)}, u32[]{:S(2)}) collective-permute-start(bf16[64,128]{1,0:T(8,128)(2,1)S(1)} %get-tuple-element.25), channel_id=1, source_target_pairs={{16,0},{24,8},{32,16},{40,24},{48,32},{56,40},{64,48},{72,56},{80,... | collective-permute-start | bytes 49160 | tf_op jit(solution)/shard_map/ppermute | solution.py:15
  82.1 4.0 %fusion.35 = (bf16[640,512]{1,0:T(8,128)(2,1)S(1)}, f32[640,512]{1,0:T(8,128)}) fusion(f32[640,512]{1,0:T(8,128)S(1)} %fusion.10, bf16[128,16,640]{0,2,1:T(8,128)(2,1)S(1)} %fusion.2, bf16[128,16,512]{2,1,0:T(8,128)(2,1)S(1)} %copy-done), kind=kOutput, calls=%fused_computation.59 | convolution fusion | flops 1342832640 | bytes 7995392 | tf_op jit(solution)/shard_map/thk,thc->kc/dot_general | solution.py:70
  86.9 4.1 %copy.48 = bf16[128,16,512]{2,1,0:T(8,128)(2,1)} copy(bf16[128,16,512]{2,0,1:T(8,128)(2,1)} %convolution_convert_fusion) | data formatting | bytes 4194304
  91.0 2.3 %collective-permute-start.8 = (bf16[128,512]{1,0:T(8,128)(2,1)S(1)}, bf16[128,512]{1,0:T(8,128)(2,1)S(1)}, u32[]{:S(2)}, u32[]{:S(2)}) collective-permute-start(bf16[128,512]{1,0:T(8,128)(2,1)S(1)} %get-tuple-element.18), channel_id=1, source_target_pairs={{8,0},{16,8},{24,16},{32,24},{40,32},{48,40},{56,48},{64,56},{72,6... | collective-permute-start | bytes 393224 | tf_op jit(solution)/shard_map/ppermute | solution.py:15
  93.3 2.0 %collective-permute-start.11 = (bf16[128,512]{1,0:T(8,128)(2,1)S(1)}, bf16[128,512]{1,0:T(8,128)(2,1)S(1)}, u32[]{:S(2)}, u32[]{:S(2)}) collective-permute-start(bf16[128,512]{1,0:T(8,128)(2,1)S(1)} %get-tuple-element.19), channel_id=1, source_target_pairs={{32,0},{40,8},{48,16},{56,24},{64,32},{72,40},{80,48},{88,56},{96,... | collective-permute-start | bytes 393224 | tf_op jit(solution)/shard_map/ppermute | solution.py:15
  95.3 1.9 %collective-permute-start.10 = (bf16[128,512]{1,0:T(8,128)(2,1)S(1)}, bf16[128,512]{1,0:T(8,128)(2,1)S(1)}, u32[]{:S(2)}, u32[]{:S(2)}) collective-permute-start(bf16[128,512]{1,0:T(8,128)(2,1)S(1)} %get-tuple-element.20), channel_id=1, source_target_pairs={{24,0},{32,8},{40,16},{48,24},{56,32},{64,40},{72,48},{80,56},{88,... | collective-permute-start | bytes 393224 | tf_op jit(solution)/shard_map/ppermute | solution.py:15
  97.3 2.2 %collective-permute-start.9 = (bf16[128,512]{1,0:T(8,128)(2,1)S(1)}, bf16[128,512]{1,0:T(8,128)(2,1)S(1)}, u32[]{:S(2)}, u32[]{:S(2)}) collective-permute-start(bf16[128,512]{1,0:T(8,128)(2,1)S(1)} %get-tuple-element.21), channel_id=1, source_target_pairs={{16,0},{24,8},{32,16},{40,24},{48,32},{56,40},{64,48},{72,56},{80,... | collective-permute-start | bytes 393224 | tf_op jit(solution)/shard_map/ppermute | solution.py:15
  99.6 4.9 %collective-permute-done.11 = bf16[128,512]{1,0:T(8,128)(2,1)S(1)} collective-permute-done((bf16[128,512]{1,0:T(8,128)(2,1)S(1)}, bf16[128,512]{1,0:T(8,128)(2,1)S(1)}, u32[]{:S(2)}, u32[]{:S(2)}) %collective-permute-start.11) | collective-permute-done | bytes 131104 | tf_op jit(solution)/shard_map/ppermute | solution.py:15
  104.4 2.5 %collective-permute-done.10 = bf16[128,512]{1,0:T(8,128)(2,1)S(1)} collective-permute-done((bf16[128,512]{1,0:T(8,128)(2,1)S(1)}, bf16[128,512]{1,0:T(8,128)(2,1)S(1)}, u32[]{:S(2)}, u32[]{:S(2)}) %collective-permute-start.10) | collective-permute-done | bytes 131104 | tf_op jit(solution)/shard_map/ppermute | solution.py:15
  107.0 3.8 %collective-permute-done.9 = bf16[128,512]{1,0:T(8,128)(2,1)S(1)} collective-permute-done((bf16[128,512]{1,0:T(8,128)(2,1)S(1)}, bf16[128,512]{1,0:T(8,128)(2,1)S(1)}, u32[]{:S(2)}, u32[]{:S(2)}) %collective-permute-start.9) | collective-permute-done | bytes 131104 | tf_op jit(solution)/shard_map/ppermute | solution.py:15
  111.8 46.5 %all-reduce.2 = (bf16[128,512]{1,0:T(8,128)(2,1)}, bf16[64,128]{1,0:T(8,128)(2,1)}) all-reduce(f32[128,512]{1,0:T(8,128)S(1)} %fusion.25, f32[64,128]{1,0:T(8,128)S(1)} %fusion.31), channel_id=1, replica_groups=mesh['ctx'=32,'head'=8] {'head'}, use_global_device_ids=true, to_apply=%region_6.7 | all-reduce | flops 73728 | bytes 442368 | tf_op jit(solution)/shard_map/psum | solution.py:89
  (50 shorter events, 6.7 us)
Async XLA Ops:
  0.6 39.9 %copy-start = (bf16[128,16,512]{2,1,0:T(8,128)(2,1)S(1)}, bf16[128,16,512]{2,1,0:T(8,128)(2,1)}, u32[]{:S(2)}) copy-start(bf16[128,16,512]{2,1,0:T(8,128)(2,1)} %param.6) | copy-start | bytes 6291460
  0.6 28.2 %collective-permute-start.6 = (bf16[64,128]{1,0:T(8,128)(2,1)}, bf16[64,128]{1,0:T(8,128)(2,1)S(1)}, u32[]{:S(2)}, u32[]{:S(2)}) collective-permute-start(bf16[64,128]{1,0:T(8,128)(2,1)} %param.9), channel_id=1, source_target_pairs={{0,24},{8,32},{16,40},{24,48},{32,56},{40,64},{48,72},{56,80},{64,... | collective-permute-start | bytes 49160 | tf_op jit(solution)/shard_map/ppermute | solution.py:15
  4.1 22.8 %collective-permute-start.5 = (bf16[64,128]{1,0:T(8,128)(2,1)}, bf16[64,128]{1,0:T(8,128)(2,1)S(1)}, u32[]{:S(2)}, u32[]{:S(2)}) collective-permute-start(bf16[64,128]{1,0:T(8,128)(2,1)} %param.9), channel_id=1, source_target_pairs={{0,16},{8,24},{16,32},{24,40},{32,48},{40,56},{48,64},{56,72},{64,... | collective-permute-start | bytes 49160 | tf_op jit(solution)/shard_map/ppermute | solution.py:15
  7.9 16.0 %collective-permute-start.4 = (bf16[64,128]{1,0:T(8,128)(2,1)}, bf16[64,128]{1,0:T(8,128)(2,1)S(1)}, u32[]{:S(2)}, u32[]{:S(2)}) collective-permute-start(bf16[64,128]{1,0:T(8,128)(2,1)} %param.9), channel_id=1, source_target_pairs={{0,8},{8,16},{16,24},{24,32},{32,40},{40,48},{48,56},{56,64},{64,7... | collective-permute-start | bytes 49160 | tf_op jit(solution)/shard_map/ppermute | solution.py:15
  11.6 19.5 %collective-permute-start.7 = (bf16[64,128]{1,0:T(8,128)(2,1)}, bf16[64,128]{1,0:T(8,128)(2,1)S(1)}, u32[]{:S(2)}, u32[]{:S(2)}) collective-permute-start(bf16[64,128]{1,0:T(8,128)(2,1)} %param.9), channel_id=1, source_target_pairs={{0,32},{8,40},{16,48},{24,56},{32,64},{40,72},{48,80},{56,88},{64,... | collective-permute-start | bytes 49160 | tf_op jit(solution)/shard_map/ppermute | solution.py:15
  17.1 18.9 %collective-permute-start.2 = (bf16[128,512]{1,0:T(8,128)(2,1)}, bf16[128,512]{1,0:T(8,128)(2,1)S(1)}, u32[]{:S(2)}, u32[]{:S(2)}) collective-permute-start(bf16[128,512]{1,0:T(8,128)(2,1)} %param.8), channel_id=1, source_target_pairs={{0,24},{8,32},{16,40},{24,48},{32,56},{40,64},{48,72},{56,80},{64,... | collective-permute-start | bytes 393224 | tf_op jit(solution)/shard_map/ppermute | solution.py:15
  23.9 12.0 %collective-permute-start.1 = (bf16[128,512]{1,0:T(8,128)(2,1)}, bf16[128,512]{1,0:T(8,128)(2,1)S(1)}, u32[]{:S(2)}, u32[]{:S(2)}) collective-permute-start(bf16[128,512]{1,0:T(8,128)(2,1)} %param.8), channel_id=1, source_target_pairs={{0,16},{8,24},{16,32},{24,40},{32,48},{40,56},{48,64},{56,72},{64,... | collective-permute-start | bytes 393224 | tf_op jit(solution)/shard_map/ppermute | solution.py:15
  26.9 9.0 %collective-permute-start = (bf16[128,512]{1,0:T(8,128)(2,1)}, bf16[128,512]{1,0:T(8,128)(2,1)S(1)}, u32[]{:S(2)}, u32[]{:S(2)}) collective-permute-start(bf16[128,512]{1,0:T(8,128)(2,1)} %param.8), channel_id=1, source_target_pairs={{0,8},{8,16},{16,24},{24,32},{32,40},{40,48},{48,56},{56,64},{64,7... | collective-permute-start | bytes 393224 | tf_op jit(solution)/shard_map/ppermute | solution.py:15
  28.8 11.6 %collective-permute-start.3 = (bf16[128,512]{1,0:T(8,128)(2,1)}, bf16[128,512]{1,0:T(8,128)(2,1)S(1)}, u32[]{:S(2)}, u32[]{:S(2)}) collective-permute-start(bf16[128,512]{1,0:T(8,128)(2,1)} %param.8), channel_id=1, source_target_pairs={{0,32},{8,40},{16,48},{24,56},{32,64},{40,72},{48,80},{56,88},{64,... | collective-permute-start | bytes 393224 | tf_op jit(solution)/shard_map/ppermute | solution.py:15
  48.4 3.3 %copy-start.1 = (bf16[128,16,512]{2,1,0:T(8,128)(2,1)S(1)}, bf16[128,16,512]{2,1,0:T(8,128)(2,1)}, u32[]{:S(2)}) copy-start(bf16[128,16,512]{2,1,0:T(8,128)(2,1)} %param.10) | copy-start | bytes 6291460
  51.6 6.9 %slice-start = ((s8[5242880]{0:T(1024)(128)(4,1)}), s8[4194304]{0:T(1024)(128)(4,1)S(1)}, s32[]{:S(2)}) async-start(s8[5242880]{0:T(1024)(128)(4,1)} %bitcast.47), calls=%async_computation | async-start | bytes 8388608
  55.7 2.9 %slice-start.1 = ((s8[5242880]{0:T(1024)(128)(4,1)}), s8[1048576]{0:T(1024)(128)(4,1)S(1)}, s32[]{:S(2)}) async-start(s8[5242880]{0:T(1024)(128)(4,1)} %bitcast.47), calls=%async_computation.1 | async-start | bytes 2097152
  67.6 25.7 %collective-permute-start.12 = (bf16[64,128]{1,0:T(8,128)(2,1)S(1)}, bf16[64,128]{1,0:T(8,128)(2,1)S(1)}, u32[]{:S(2)}, u32[]{:S(2)}) collective-permute-start(bf16[64,128]{1,0:T(8,128)(2,1)S(1)} %get-tuple-element.22), channel_id=1, source_target_pairs={{8,0},{16,8},{24,16},{32,24},{40,32},{48,40},{56,48},{64,56},{72,6... | collective-permute-start | bytes 49160 | tf_op jit(solution)/shard_map/ppermute | solution.py:15
  72.3 23.0 %collective-permute-start.15 = (bf16[64,128]{1,0:T(8,128)(2,1)S(1)}, bf16[64,128]{1,0:T(8,128)(2,1)S(1)}, u32[]{:S(2)}, u32[]{:S(2)}) collective-permute-start(bf16[64,128]{1,0:T(8,128)(2,1)S(1)} %get-tuple-element.23), channel_id=1, source_target_pairs={{32,0},{40,8},{48,16},{56,24},{64,32},{72,40},{80,48},{88,56},{96,... | collective-permute-start | bytes 49160 | tf_op jit(solution)/shard_map/ppermute | solution.py:15
  75.8 21.5 %collective-permute-start.14 = (bf16[64,128]{1,0:T(8,128)(2,1)S(1)}, bf16[64,128]{1,0:T(8,128)(2,1)S(1)}, u32[]{:S(2)}, u32[]{:S(2)}) collective-permute-start(bf16[64,128]{1,0:T(8,128)(2,1)S(1)} %get-tuple-element.24), channel_id=1, source_target_pairs={{24,0},{32,8},{40,16},{48,24},{56,32},{64,40},{72,48},{80,56},{88,... | collective-permute-start | bytes 49160 | tf_op jit(solution)/shard_map/ppermute | solution.py:15
  80.1 19.5 %collective-permute-start.13 = (bf16[64,128]{1,0:T(8,128)(2,1)S(1)}, bf16[64,128]{1,0:T(8,128)(2,1)S(1)}, u32[]{:S(2)}, u32[]{:S(2)}) collective-permute-start(bf16[64,128]{1,0:T(8,128)(2,1)S(1)} %get-tuple-element.25), channel_id=1, source_target_pairs={{16,0},{24,8},{32,16},{40,24},{48,32},{56,40},{64,48},{72,56},{80,... | collective-permute-start | bytes 49160 | tf_op jit(solution)/shard_map/ppermute | solution.py:15
  91.0 8.6 %collective-permute-start.8 = (bf16[128,512]{1,0:T(8,128)(2,1)S(1)}, bf16[128,512]{1,0:T(8,128)(2,1)S(1)}, u32[]{:S(2)}, u32[]{:S(2)}) collective-permute-start(bf16[128,512]{1,0:T(8,128)(2,1)S(1)} %get-tuple-element.18), channel_id=1, source_target_pairs={{8,0},{16,8},{24,16},{32,24},{40,32},{48,40},{56,48},{64,56},{72,6... | collective-permute-start | bytes 393224 | tf_op jit(solution)/shard_map/ppermute | solution.py:15
  93.3 11.1 %collective-permute-start.11 = (bf16[128,512]{1,0:T(8,128)(2,1)S(1)}, bf16[128,512]{1,0:T(8,128)(2,1)S(1)}, u32[]{:S(2)}, u32[]{:S(2)}) collective-permute-start(bf16[128,512]{1,0:T(8,128)(2,1)S(1)} %get-tuple-element.19), channel_id=1, source_target_pairs={{32,0},{40,8},{48,16},{56,24},{64,32},{72,40},{80,48},{88,56},{96,... | collective-permute-start | bytes 393224 | tf_op jit(solution)/shard_map/ppermute | solution.py:15
  95.3 11.6 %collective-permute-start.10 = (bf16[128,512]{1,0:T(8,128)(2,1)S(1)}, bf16[128,512]{1,0:T(8,128)(2,1)S(1)}, u32[]{:S(2)}, u32[]{:S(2)}) collective-permute-start(bf16[128,512]{1,0:T(8,128)(2,1)S(1)} %get-tuple-element.20), channel_id=1, source_target_pairs={{24,0},{32,8},{40,16},{48,24},{56,32},{64,40},{72,48},{80,56},{88,... | collective-permute-start | bytes 393224 | tf_op jit(solution)/shard_map/ppermute | solution.py:15
  97.3 13.5 %collective-permute-start.9 = (bf16[128,512]{1,0:T(8,128)(2,1)S(1)}, bf16[128,512]{1,0:T(8,128)(2,1)S(1)}, u32[]{:S(2)}, u32[]{:S(2)}) collective-permute-start(bf16[128,512]{1,0:T(8,128)(2,1)S(1)} %get-tuple-element.21), channel_id=1, source_target_pairs={{16,0},{24,8},{32,16},{40,24},{48,32},{56,40},{64,48},{72,56},{80,... | collective-permute-start | bytes 393224 | tf_op jit(solution)/shard_map/ppermute | solution.py:15
where the time goes:
time: 159 us; the launch traced here: 158 us
  starting transfers between devices  48.8 us (31%)
  blocking collectives  46.5 us (29%)
  matrix products  30.9 us (19%)
  waiting for transfers between devices  17.4 us (11%)
  local copies, waits for them, and re-layouts  8.6 us (5%)
  other arithmetic  5.01 us (3%)
    ppermute x16, starting transfers between devices, from_behind(): return lax.ppermute(shard, axis, pairs)  48.8 us
    psum x1, blocking collectives, local(): summed_lat, summed_rope = lax.psum((total_lat, total_rope), 'head')  46.5 us
    ppermute x16, waiting for transfers between devices, from_behind(): return lax.ppermute(shard, axis, pairs)  17.4 us
    sub x1, matrix products, local(): weights_exp = jnp.exp(scores - row_max)  7.87 us
    unnamed x19, local copies, waits for them, and re-layouts  7.8 us
    dot_general x1, matrix products, local(): jnp.einsum('thc,kc->thk', out_grad, key_lat, preferred_element_type=jnp.f...  4.32 us
    dot_general x1, matrix products, local(): jnp.einsum('thk,kc->thc', probs_b, key_lat, preferred_element_type=jnp.fl...  4.05 us
    dot_general x1, matrix products, local(): jnp.einsum('thk,thc->kc', score_grad, query_latent, preferred_element_typ...  3.98 us
  transfers between devices with their start and end apart: 16, of which 5 were waited for; matrix products, arithmetic and copies ran while one was open for 10% of the time, Pallas kernels for 0%

commit v1 on v0

v1 whole, which is shorter than its diff:
```python
import functools
import math

import jax
import jax.numpy as jnp
from jax import lax
from jax.experimental import pallas as pl
from jax.experimental.pallas import tpu as pltpu
from jax.sharding import PartitionSpec as P

MESH = pl.DeviceIdType.MESH
SPAN = 4
SLOTS = SPAN + 1
QUARTERS = 4
LANES = 128
TILE = 256
softmax_scale = 192.0 ** (-0.5)
exp2_scale = softmax_scale * math.log2(math.e)
f32 = jnp.float32
bf16 = jnp.bfloat16


def kernel(
    n_ctx,
    heads,
    len_ref,
    q_hbm,
    do_hbm,
    qr_ref,
    lat_ref,
    rope_ref,
    dq_hbm,
    dqr_ref,
    dlat_ref,
    drope_ref,
    q_v,
    do_v,
    q_t,
    do_t,
    qr_f,
    qr_v,
    s_v,
    dp_v,
    p_t,
    ds_t,
    dq_v,
    kbuf,
    kcat,
    k_t,
    gbuf,
    r1,
    s2,
    r2,
    v3,
    s3,
    r3,
    s4,
    r4,
    obuf,
    in_sem,
    out_sem,
    zs,
    zr,
    y1s,
    y1r,
    y2s,
    y2r,
    cs,
    cr,
    a1s,
    a1r,
    a2s,
    a2r,
    a3s,
    a3r,
    a4s,
    a4r,
    fxs,
    fxr,
    f1s,
    f1r,
    f2s,
    f2r,
):
    rows, width = q_v.shape
    tok = lat_ref.shape[0]
    rope = rope_ref.shape[0]
    tiles = rows // TILE
    krows = kbuf.shape[2]
    part = r3.shape[1]
    rest = krows - part

    ctx = lax.axis_index("ctx")
    head = lax.axis_index("head")
    core = ctx % 2
    y = head // 2
    xh = head % 2
    y_a = y + 1 - 2 * (y % 2)
    y_b = 3 - y
    y_opp = (y + 2) % 4
    y_p1 = y_a * (1 - core) + y_b * core
    y_p2 = y_b * (1 - core) + y_a * core
    here = (ctx, head)
    p1 = (ctx, y_p1 * 2 + xh)
    p2 = (ctx, y_p2 * 2 + xh)
    px = (ctx, y * 2 + 1 - xh)
    sib = (ctx + 1 - 2 * core, head)

    def along(by):
        return ((ctx + by + n_ctx) % n_ctx, head)

    def remote(src, dst, send, recv, to):
        return pltpu.make_async_remote_copy(
            src_ref=src, dst_ref=dst, send_sem=send, recv_sem=recv, device_id=to, device_id_type=MESH
        )

    in_q = pltpu.make_async_copy(q_hbm, q_v, in_sem.at[0])
    in_do = pltpu.make_async_copy(do_hbm, do_v, in_sem.at[1])
    in_q.start()
    in_do.start()

    barrier = pltpu.get_barrier_semaphore()
    peers = [p1, p2, px] + [along(by) for by in (-4, -3, -2, -1, 1, 2, 3, 4)]
    for peer in peers:
        pl.semaphore_signal(barrier, inc=1, device_id=peer, device_id_type=MESH)

    def own_keys():
        for q in range(QUARTERS):
            kbuf[0, q, :tok, :] = lat_ref[:, q * LANES : (q + 1) * LANES]
            kbuf[0, q, tok:, :] = rope_ref[q * 16 : (q + 1) * 16, :]

    own_keys()
    pl.semaphore_wait(barrier, len(peers))

    def z_copy(n):
        slot = 2 + 2 * n
        return remote(kbuf.at[0, y], kbuf.at[slot, y], zs.at[n], zr.at[n], along(slot))

    def y1_copy(n):
        slot = 2 + 2 * n
        return remote(kbuf.at[slot, y], kbuf.at[slot, y], y1s.at[n], y1r.at[n], p1)

    def y2_copy(n, k):
        slot = 2 + 2 * n
        quarter = (y, y_p1)[k]
        return remote(
            kbuf.at[slot, quarter], kbuf.at[slot, quarter], y2s.at[n, k], y2r.at[n, k], p2
        )

    def core_copy(src, n):
        return remote(kbuf.at[src], kbuf.at[1 + 2 * n], cs.at[n], cr.at[n], sib)

    z_copy(0).start()
    z_copy(1).start()

    @pl.when(core == 0)
    def _():
        core_copy(0, 0).start()

    def after_z(n):
        z_copy(n).wait_recv()
        y1_copy(n).start()

    def after_y1(n):
        y1_copy(n).wait_recv()
        y2_copy(n, 0).start()
        y2_copy(n, 1).start()

    def after_y2(n):
        y2_copy(n, 0).wait_recv()
        y2_copy(n, 1).wait_recv()
        if n == 0:

            @pl.when(core == 0)
            def _():
                core_copy(2, 1).start()

            @pl.when(core == 1)
            def _():
                core_copy(2, 0).start()
        else:

            @pl.when(core == 1)
            def _():
                core_copy(4, 1).start()

    def unpack(slot):
        at = slot * tok
        wide = jnp.concatenate([kbuf[slot, q, :tok, :] for q in range(QUARTERS)], axis=1)
        turned = jnp.concatenate([kbuf[slot, q, tok:, :] for q in range(QUARTERS)], axis=0)
        kcat[at : at + tok, :width] = wide
        padded = jnp.concatenate([turned, jnp.zeros((LANES - rope, tok), bf16)], axis=0)
        kcat[at : at + tok, width:] = padded.T
        k_t[:width, at : at + tok] = wide.T
        k_t[width:, at : at + tok] = turned

    def lanes(i):
        return pl.ds(pl.multiple_of(i * TILE, TILE), TILE)

    def turn_q(i, c):
        q_t[:width, lanes(i)] = q_v[lanes(i), :].T
        return c

    def turn_do(i, c):
        do_t[:, lanes(i)] = do_v[lanes(i), :].T
        return c

    def turn_rope(i, c):
        block = qr_f[lanes(i), :].astype(bf16)
        qr_v[lanes(i), :] = block
        q_t[width:, lanes(i)] = block.T
        return c

    def scores(first, count):
        def body(i, c):
            at = first * tok
            keys = kcat[at : at + count * tok, :]
            s_v[at : at + count * tok, lanes(i)] = jnp.dot(
                keys, q_t[:, lanes(i)], preferred_element_type=f32
            )
            dp_v[at : at + count * tok, lanes(i)] = jnp.dot(
                keys[:, :width], do_t[:, lanes(i)], preferred_element_type=f32
            )
            return c

        lax.fori_loop(0, tiles, body, 0)

    in_q.wait()
    lax.fori_loop(0, tiles, turn_q, 0)
    qr_f[...] = jnp.zeros_like(qr_f)
    for h in range(heads):
        qr_f[pl.ds(h, tok, stride=heads), :rope] = qr_ref[:, h * rope : (h + 1) * rope].astype(f32)
    lax.fori_loop(0, tiles, turn_rope, 0)
    after_z(0)
    unpack(0)
    in_do.wait()
    lax.fori_loop(0, tiles, turn_do, 0)
    after_y1(0)
    after_z(1)
    scores(0, 1)
    after_y2(0)
    after_y1(1)
    unpack(2)
    after_y2(1)
    core_copy(0, 0).wait_recv()
    unpack(1)
    scores(1, 2)
    unpack(4)
    core_copy(0, 1).wait_recv()
    unpack(3)
    scores(3, 2)

    ends = []
    total = jnp.int32(0)
    for k in range(len_ref.shape[0]):
        total = total + len_ref[k]
        ends.append(total - ctx * tok)

    def softmax(i, c):
        sl = lanes(i)
        token = (lax.broadcasted_iota(jnp.int32, (1, TILE), 1) + i * TILE) // heads
        low = jnp.full((1, TILE), -ctx * tok, jnp.int32)
        for end in ends:
            low = jnp.maximum(low, jnp.where(end <= token, end, low))
        key = lax.broadcasted_iota(jnp.int32, (tok, TILE), 0)
        top = jnp.full((1, TILE), -jnp.inf, f32)
        for d in range(SLOTS):
            at = pl.ds(d * tok, tok)
            ok = key >= low + d * tok
            if d == 0:
                ok = ok & (key <= token)
            s = jnp.where(ok, s_v[at, sl], -jnp.inf)
            s_v[at, sl] = s
            top = jnp.maximum(top, jnp.max(s, axis=0, keepdims=True))
        norm = jnp.zeros((1, TILE), f32)
        for d in range(SLOTS):
            at = pl.ds(d * tok, tok)
            e = jnp.exp2((s_v[at, sl] - top) * exp2_scale)
            s_v[at, sl] = e
            norm = norm + jnp.sum(e, axis=0, keepdims=True)
        inverse = 1.0 / norm
        delta = jnp.zeros((1, TILE), f32)
        for d in range(SLOTS):
            at = pl.ds(d * tok, tok)
            pb = (s_v[at, sl] * inverse).astype(bf16)
            p_t[at, sl] = pb
            delta = delta + jnp.sum(pb.astype(f32) * dp_v[at, sl], axis=0, keepdims=True)
        scaled = inverse * softmax_scale
        for d in range(SLOTS):
            at = pl.ds(d * tok, tok)
            ds_t[at, sl] = (s_v[at, sl] * scaled * (dp_v[at, sl] - delta)).astype(bf16)
        return c

    lax.fori_loop(0, tiles, softmax, 0)

    def key_terms(first, count):
        at = pl.ds(first * tok, count * tok)
        g = jnp.dot(p_t[at, :], do_v[...], preferred_element_type=f32)
        g = g + jnp.dot(ds_t[at, :], q_v[...], preferred_element_type=f32)
        gr = jnp.dot(ds_t[at, :], qr_v[...], preferred_element_type=f32)
        for k in range(count):
            piece = slice(k * tok, (k + 1) * tok)
            turned = gr[piece, :].T
            for q in range(QUARTERS):
                gbuf[first + k, q, :tok, :] = g[piece, q * LANES : (q + 1) * LANES].astype(bf16)
                gbuf[first + k, q, tok:, :] = turned[q * 16 : (q + 1) * 16, :].astype(bf16)

    def a1_copy(d, k):
        return remote(gbuf.at[d, (y_p1, y_opp)[k]], r1.at[d, k], a1s.at[d, k], a1r.at[d, k], p1)

    def a2_copy(d):
        return remote(s2.at[d], r2.at[d], a2s.at[d], a2r.at[d], p2)

    def a3_copy(d):
        away = pl.ds(pl.multiple_of(rest * (1 - xh), 16), part)
        return remote(s3.at[d, away], r3.at[d], a3s.at[d], a3r.at[d], px)

    def a4_copy(d):
        return remote(s4.at[d], r4.at[d], a4s.at[d], a4r.at[d], along(-d))

    def red1(d):
        a1_copy(d, 1).start()
        a1_copy(d, 0).start()

    def red2(d):
        a1_copy(d, 1).wait_recv()
        s2[d] = (gbuf[d, y_p2].astype(f32) + r1[d, 1].astype(f32)).astype(bf16)
        a2_copy(d).start()
        a1_copy(d, 0).wait_recv()

    def red3(d):
        mine = gbuf[d, y].astype(f32) + r1[d, 0].astype(f32)
        a2_copy(d).wait_recv()
        s3[d] = (mine + r2[d].astype(f32)).astype(bf16)
        a3_copy(d).start()

    near = pl.ds(pl.multiple_of(rest * xh, 16), part)

    def red4(d):
        a3_copy(d).wait_recv()
        both = s3[d, near].astype(f32) + r3[d].astype(f32)
        if d == 0:
            v3[...] = both
        else:
            s4[d] = both.astype(bf16)
            a4_copy(d).start()

    def fx_copy():
        whole = pl.ds(pl.multiple_of(part * xh, 16), rest)
        return remote(obuf.at[y, whole], obuf.at[y, whole], fxs, fxr, px)

    def fx_arrival():
        whole = pl.ds(pl.multiple_of(part * (1 - xh), 16), rest)
        return remote(obuf.at[y, whole], obuf.at[y, whole], fxs, fxr, px)

    def f1_copy():
        return remote(obuf.at[y], obuf.at[y], f1s, f1r, p1)

    def f2_copy(k):
        quarter = (y, y_p1)[k]
        return remote(obuf.at[quarter], obuf.at[quarter], f2s.at[k], f2r.at[k], p2)

    def out_copy(i):
        return pltpu.make_async_copy(dq_v.at[lanes(i)], dq_hbm.at[lanes(i)], out_sem.at[i])

    def query_terms(i, c):
        sl = lanes(i)
        turned = jnp.dot(k_t[...], ds_t[:, sl], preferred_element_type=f32)
        dq_v[sl, :] = turned[:width, :].astype(bf16).T
        qr_f[sl, :rope] = turned[width:, :].T
        out_copy(i).start()
        return c

    def query_run(first, last):
        lax.fori_loop(first, last, query_terms, 0)

    key_terms(3, 2)
    red1(4)
    red1(3)
    key_terms(1, 2)
    red1(2)
    red1(1)
    red2(4)
    red2(3)
    key_terms(0, 1)
    red1(0)
    red3(4)
    red3(3)
    red2(2)
    red2(1)
    quarter = tiles // 4
    query_run(0, quarter)
    red2(0)
    red4(4)
    red4(3)
    red3(2)
    red3(1)
    query_run(quarter, 2 * quarter)
    red3(0)
    red4(2)
    red4(1)
    query_run(2 * quarter, 3 * quarter)
    red4(0)
    query_run(3 * quarter, tiles)
    for h in range(heads):
        dqr_ref[:, h * rope : (h + 1) * rope] = qr_f[pl.ds(h, tok, stride=heads), :rope].astype(bf16)

    total_grad = v3[...]
    for d in range(1, SLOTS):
        a4_copy(d).wait_recv()
        total_grad = total_grad + r4[d].astype(f32)
    obuf[y, near] = total_grad.astype(bf16)
    fx_copy().start()
    fx_arrival().wait_recv()
    f1_copy().start()
    f1_copy().wait_recv()
    f2_copy(0).start()
    f2_copy(1).start()
    f2_copy(0).wait_recv()
    f2_copy(1).wait_recv()
    for q in range(QUARTERS):
        dlat_ref[:, q * LANES : (q + 1) * LANES] = obuf[q, :tok, :]
        drope_ref[q * 16 : (q + 1) * 16, :] = obuf[q, tok:, :]

    for i in range(tiles):
        out_copy(i).wait()
    for n in range(2):
        z_copy(n).wait_send()
        y1_copy(n).wait_send()
        y2_copy(n, 0).wait_send()
        y2_copy(n, 1).wait_send()
        core_copy(0, n).wait_send()
        f2_copy(n).wait_send()
    for d in range(SLOTS):
        a1_copy(d, 0).wait_send()
        a1_copy(d, 1).wait_send()
        a2_copy(d).wait_send()
        a3_copy(d).wait_send()
        if d:
            a4_copy(d).wait_send()
    fx_copy().wait_send()
    f1_copy().wait_send()


def local(query_latent, query_rope, latent, rope_key, out_grad, doc_lengths, n_ctx):
    tok, heads, width = query_latent.shape
    rope = rope_key.shape[0]
    rows = tok * heads
    keys = SLOTS * tok
    krows = tok + rope * tok // width
    half = (krows // 2 + 15) // 16 * 16
    dma = pltpu.SemaphoreType.DMA
    vmem = pltpu.VMEM
    in_vmem = pl.BlockSpec(memory_space=pltpu.VMEM)
    in_any = pl.BlockSpec(memory_space=pl.ANY)
    dq, dqr, dlat, drope = pl.pallas_call(
        functools.partial(kernel, n_ctx, heads),
        out_shape=(
            jax.ShapeDtypeStruct((rows, width), bf16),
            jax.ShapeDtypeStruct((tok, heads * rope), bf16),
            jax.ShapeDtypeStruct((tok, width), bf16),
            jax.ShapeDtypeStruct((rope, tok), bf16),
        ),
        in_specs=[pl.BlockSpec(memory_space=pltpu.SMEM), in_any, in_any, in_vmem, in_vmem, in_vmem],
        out_specs=(in_any, in_vmem, in_vmem, in_vmem),
        scratch_shapes=[
            vmem((rows, width), bf16),
            vmem((rows, width), bf16),
            vmem((width + LANES, rows), bf16),
            vmem((width, rows), bf16),
            vmem((rows, LANES), f32),
            vmem((rows, LANES), bf16),
            vmem((keys, rows), f32),
            vmem((keys, rows), f32),
            vmem((keys, rows), bf16),
            vmem((keys, rows), bf16),
            vmem((rows, width), bf16),
            vmem((SLOTS, QUARTERS, krows, LANES), bf16),
            vmem((keys, width + LANES), bf16),
            vmem((width + rope, keys), bf16),
            vmem((SLOTS, QUARTERS, krows, LANES), bf16),
            vmem((SLOTS, 2, krows, LANES), bf16),
            vmem((SLOTS, krows, LANES), bf16),
            vmem((SLOTS, krows, LANES), bf16),
            vmem((half, LANES), f32),
            vmem((SLOTS, krows, LANES), bf16),
            vmem((SLOTS, half, LANES), bf16),
            vmem((SLOTS, half, LANES), bf16),
            vmem((SLOTS, half, LANES), bf16),
            vmem((QUARTERS, krows, LANES), bf16),
            dma((2,)),
            dma((rows // TILE,)),
            dma((2,)),
            dma((2,)),
            dma((2,)),
            dma((2,)),
            dma((2, 2)),
            dma((2, 2)),
            dma((2,)),
            dma((2,)),
            dma((SLOTS, 2)),
            dma((SLOTS, 2)),
            dma((SLOTS,)),
            dma((SLOTS,)),
            dma((SLOTS,)),
            dma((SLOTS,)),
            dma((SLOTS,)),
            dma((SLOTS,)),
            dma,
            dma,
            dma,
            dma,
            dma((2,)),
            dma((2,)),
        ],
        compiler_params=pltpu.CompilerParams(
            collective_id=0, has_side_effects=True, vmem_limit_bytes=56 * 1024 * 1024
        ),
    )(
        doc_lengths,
        query_latent.reshape(rows, width),
        out_grad.reshape(rows, width),
        query_rope,
        latent,
        rope_key,
    )
    return dq.reshape(tok, heads, width), dqr, dlat, drope


def solution(mesh):
    in_specs = (
        P("ctx", "head", None),
        P("ctx", "head"),
        P("ctx", None),
        P(None, "ctx"),
        P("ctx", "head", None),
        P(),
    )
    out_specs = (P("ctx", "head", None), P("ctx", "head"), P("ctx", None), P(None, "ctx"))
    return jax.shard_map(
        functools.partial(local, n_ctx=mesh.shape["ctx"]),
        mesh=mesh,
        in_specs=in_specs,
        out_specs=out_specs,
        check_vma=False,
    )
```

time: 159 us -> 70.7 us (0.44)
  the two profiles are of different devices: /device:TPU:2 before, /device:TPU:24 now
where the time goes in v1:
time: 70.7 us; the launch traced here: 70.6 us
  Pallas kernels  64.8 us (92%)
  local copies, waits for them, and re-layouts  5.1 us (7%)
    pallas_call x1, Pallas kernels, local(): pl.pallas_call(functools.partial(kernel, n_ctx, heads), out_shape=(jax.Sh...  64.8 us
    unnamed x10, local copies, waits for them, and re-layouts  5.1 us

profile of v1, /device:TPU:24, one launch (start us, length us, event | category | flops | bytes accessed | tf_op | source)
XLA Modules:
  0.0 70.6 jit_solution(12733136937358786643)
XLA Ops:
  0.6 64.8 %shard_map.93 = (bf16[2048,512]{1,0:T(8,128)(2,1)}, bf16[128,1024]{1,0:T(8,128)(2,1)}, bf16[128,512]{1,0:T(8,128)(2,1)}, bf16[64,128]{1,0:T(8,128)(2,1)}) custom-call(s32[16]{0:T(128)} %len_ref.1, bf16[2048,512]{1,0:T(8,128)(2,1)} %bitcast.3, bf16[2048,512]{1,0:T(8,128)(2,1)} %bitcast.4, bf16[128,1024]{1,0:T(8,128)(2,1)} %qr_ref.1, ...), custom_call_target="tpu_custom_call" | custom-call | tf_op jit(solution)/shard_map/pallas_call | solution.py:456
  65.4 0.0 copy-start
  65.4 0.0 copy-start.1
  65.5 0.0 copy-start.2
  65.5 3.1 %copy.14 = bf16[128,16,512]{2,1,0:T(8,128)(2,1)} copy(bf16[128,16,512]{2,1,0:T(8,128)(2,1)} %bitcast.5) | data formatting | bytes 4194304
  68.6 0.0 copy-done
  68.6 0.7 copy.15
  69.3 0.0 copy-done.1
  69.3 0.7 copy.16
  70.0 0.0 copy-done.2
  70.0 0.6 copy.17
Async XLA Ops:
  65.4 3.2 %copy-start = (bf16[128,1024]{1,0:T(8,128)(2,1)S(1)}, bf16[128,1024]{1,0:T(8,128)(2,1)}, u32[]{:S(2)}) copy-start(bf16[128,1024]{1,0:T(8,128)(2,1)} %get-tuple-element.17) | copy-start | bytes 786436
  65.4 3.9 %copy-start.1 = (bf16[128,512]{1,0:T(8,128)(2,1)S(1)}, bf16[128,512]{1,0:T(8,128)(2,1)}, u32[]{:S(2)}) copy-start(bf16[128,512]{1,0:T(8,128)(2,1)} %get-tuple-element.18) | copy-start | bytes 393220
  65.5 4.5 %copy-start.2 = (bf16[64,128]{1,0:T(8,128)(2,1)S(1)}, bf16[64,128]{1,0:T(8,128)(2,1)}, u32[]{:S(2)}) copy-start(bf16[64,128]{1,0:T(8,128)(2,1)} %get-tuple-element.19) | copy-start | bytes 49156

commit v2 on v1

v2 whole, which is shorter than its diff:
```python
import functools
import math

import jax
import jax.numpy as jnp
from jax import lax
from jax.experimental import pallas as pl
from jax.experimental.pallas import tpu as pltpu
from jax.sharding import PartitionSpec as P

MESH = pl.DeviceIdType.MESH
SPAN = 4
SLOTS = SPAN + 1
BLOCKS = SPAN + 2
QUARTERS = 4
LANES = 128
TILE = 256
softmax_scale = 192.0 ** (-0.5)
exp2_scale = softmax_scale * math.log2(math.e)
f32 = jnp.float32
bf16 = jnp.bfloat16


def kernel(
    n_ctx,
    heads,
    len_ref,
    q_hbm,
    do_hbm,
    qr_ref,
    lat_ref,
    rope_ref,
    dq_hbm,
    dqr_ref,
    dlat_ref,
    drope_ref,
    q_v,
    do_v,
    q_t,
    do_t,
    qr_f,
    qr_v,
    low_v,
    top_v,
    norm_v,
    s_v,
    dp_v,
    p_t,
    ds_t,
    dq_v,
    kbuf,
    kcat,
    k_t,
    gbuf,
    rc,
    s1,
    ry,
    sz,
    rz,
    sx,
    rx,
    fo,
    obuf,
    in_sem,
    out_sem,
    zs,
    zr,
    ys,
    yr,
    cs,
    cr,
    bs,
    br,
    a1s,
    a1r,
    a2s,
    a2r,
    a3s,
    a3r,
    fs,
    fr,
):
    rows, width = q_v.shape
    tok = lat_ref.shape[0]
    rope = rope_ref.shape[0]
    tiles = rows // TILE
    krows = kbuf.shape[2]
    part = rz.shape[1]
    rest = krows - part

    ctx = lax.axis_index("ctx")
    head = lax.axis_index("head")
    core = ctx % 2
    y = head // 2
    xh = head % 2
    sib = ctx + 1 - 2 * core

    def other_y(k):
        return (y + k) % 4

    def along(by):
        return ((ctx + by + n_ctx) % n_ctx, head)

    def at_y(k, c=None):
        return (ctx if c is None else c, other_y(k) * 2 + xh)

    px = (ctx, y * 2 + 1 - xh)

    def remote(src, dst, send, recv, to):
        return pltpu.make_async_remote_copy(
            src_ref=src, dst_ref=dst, send_sem=send, recv_sem=recv, device_id=to, device_id_type=MESH
        )

    in_q = pltpu.make_async_copy(q_hbm, q_v, in_sem.at[0])
    in_do = pltpu.make_async_copy(do_hbm, do_v, in_sem.at[1])

    barrier = pltpu.get_barrier_semaphore()
    peers = [along(by) for by in (-4, -2, 2, 4)] + [px, (sib, head)]
    for k in (1, 2, 3):
        peers += [at_y(k), at_y(k, sib)]
    for peer in peers:
        pl.semaphore_signal(barrier, inc=1, device_id=peer, device_id_type=MESH)
    in_q.start()
    in_do.start()

    for q in range(QUARTERS):
        kbuf[0, q, :tok, :] = lat_ref[:, q * LANES : (q + 1) * LANES]
        kbuf[0, q, tok:, :] = rope_ref[q * 16 : (q + 1) * 16, :]
    unread = (BLOCKS - 1) * core
    gbuf[unread] = jnp.zeros(gbuf.shape[1:], bf16)
    pl.semaphore_wait(barrier, len(peers))

    def z4_copy():
        return remote(kbuf.at[0, y], kbuf.at[4, y], zs.at[1], zr.at[1], along(4))

    def z2_copy():
        return remote(kbuf.at[0], kbuf.at[2], zs.at[0], zr.at[0], along(2))

    def y_copy(k):
        return remote(kbuf.at[4, y], kbuf.at[4, y], ys.at[k - 1], yr.at[k - 1], at_y(k))

    def core_copy(src, n):
        return remote(kbuf.at[src], kbuf.at[1 + 2 * n], cs.at[n], cr.at[n], (sib, head))

    mine = pl.ds(pl.multiple_of(rest * core, 16), part)
    theirs = pl.ds(pl.multiple_of(rest * (1 - core), 16), part)

    def b_copy(d):
        b = d + 1 - core
        return remote(gbuf.at[b, :, theirs], rc.at[b], bs.at[b], br.at[b], (sib, head))

    def b_unread():
        return remote(
            gbuf.at[unread, :, theirs], rc.at[unread], bs.at[unread], br.at[unread], (sib, head)
        )

    def b_arrival(b):
        return remote(gbuf.at[b, :, theirs], rc.at[b], bs.at[b], br.at[b], (sib, head))

    z4_copy().start()
    z2_copy().start()

    @pl.when(core == 0)
    def _():
        core_copy(0, 0).start()

    b_unread().start()

    def after_z4():
        z4_copy().wait_recv()
        for k in (2, 1, 3):
            y_copy(k).start()

    def after_z2():
        z2_copy().wait_recv()

        @pl.when(core == 0)
        def _():
            core_copy(2, 1).start()

        @pl.when(core == 1)
        def _():
            core_copy(2, 0).start()

    def after_y():
        for k in (1, 2, 3):
            y_copy(k).wait_recv()

        @pl.when(core == 1)
        def _():
            core_copy(4, 1).start()

    def unpack(slot):
        at = slot * tok
        wide = jnp.concatenate([kbuf[slot, q, :tok, :] for q in range(QUARTERS)], axis=1)
        turned = jnp.concatenate([kbuf[slot, q, tok:, :] for q in range(QUARTERS)], axis=0)
        kcat[at : at + tok, :width] = wide
        padded = jnp.concatenate([turned, jnp.zeros((LANES - rope, tok), bf16)], axis=0)
        kcat[at : at + tok, width:] = padded.T
        k_t[:width, at : at + tok] = wide.T
        k_t[width:, at : at + tok] = turned

    def lanes(i):
        return pl.ds(pl.multiple_of(i * TILE, TILE), TILE)

    def token_of(i):
        return (lax.broadcasted_iota(jnp.int32, (1, TILE), 1) + i * TILE) // heads

    def turn_q(i, c):
        q_t[:width, lanes(i)] = q_v[lanes(i), :].T
        return c

    def turn_do(i, c):
        do_t[:, lanes(i)] = do_v[lanes(i), :].T
        return c

    def turn_rope(i, c):
        block = qr_f[lanes(i), :].astype(bf16)
        qr_v[lanes(i), :] = block
        q_t[width:, lanes(i)] = block.T
        return c

    ends = []
    total = jnp.int32(0)
    for k in range(len_ref.shape[0]):
        total = total + len_ref[k]
        ends.append(total - ctx * tok)

    def first_key(i, c):
        token = token_of(i)
        low = jnp.full((1, TILE), -ctx * tok, jnp.int32)
        for end in ends:
            low = jnp.maximum(low, jnp.where(end <= token, end, low))
        low_v[:, lanes(i)] = low
        return c

    def chunk(n, first, count, i):
        sl = lanes(i)
        at = pl.ds(first * tok, count * tok)
        keys = kcat[at, :]
        s = jnp.dot(keys, q_t[:, sl], preferred_element_type=f32)
        dp_v[at, sl] = jnp.dot(keys[:, :width], do_t[:, sl], preferred_element_type=f32)
        low = low_v[:, sl]
        key = lax.broadcasted_iota(jnp.int32, (tok, TILE), 0)
        masked = []
        for k in range(count):
            d = first + k
            ok = key >= low + d * tok
            if d == 0:
                ok = ok & (key <= token_of(i))
            masked.append(jnp.where(ok, s[k * tok : (k + 1) * tok], -jnp.inf))
        top = jnp.full((1, TILE), -1e30, f32)
        for m in masked:
            top = jnp.maximum(top, jnp.max(m, axis=0, keepdims=True))
        norm = jnp.zeros((1, TILE), f32)
        for k in range(count):
            e = jnp.exp2((masked[k] - top) * exp2_scale)
            s_v[pl.ds((first + k) * tok, tok), sl] = e
            norm = norm + jnp.sum(e, axis=0, keepdims=True)
        top_v[n : n + 1, sl] = top
        norm_v[n : n + 1, sl] = norm

    def finish(i):
        sl = lanes(i)
        tops = [top_v[n : n + 1, sl] for n in range(3)]
        top = jnp.maximum(jnp.maximum(tops[0], tops[1]), tops[2])
        shares = [jnp.exp2((t - top) * exp2_scale) for t in tops]
        norm = sum(shares[n] * norm_v[n : n + 1, sl] for n in range(3))
        inverse = 1.0 / norm
        weights = [share * inverse for share in shares]
        delta = jnp.zeros((1, TILE), f32)
        for d in range(SLOTS):
            at = pl.ds(d * tok, tok)
            pb = (s_v[at, sl] * weights[(d + 1) // 2]).astype(bf16)
            p_t[at, sl] = pb
            delta = delta + jnp.sum(pb.astype(f32) * dp_v[at, sl], axis=0, keepdims=True)
        for d in range(SLOTS):
            at = pl.ds(d * tok, tok)
            scaled = weights[(d + 1) // 2] * softmax_scale
            ds_t[at, sl] = (s_v[at, sl] * scaled * (dp_v[at, sl] - delta)).astype(bf16)

    def scores(n, first, count):
        def body(i, c):
            chunk(n, first, count, i)
            return c

        lax.fori_loop(0, tiles, body, 0)

    def last_scores():
        def body(i, c):
            chunk(2, 3, 2, i)
            finish(i)
            return c

        lax.fori_loop(0, tiles, body, 0)

    in_q.wait()
    lax.fori_loop(0, tiles, turn_q, 0)
    qr_f[...] = jnp.zeros_like(qr_f)
    for h in range(heads):
        qr_f[pl.ds(h, tok, stride=heads), :rope] = qr_ref[:, h * rope : (h + 1) * rope].astype(f32)
    lax.fori_loop(0, tiles, turn_rope, 0)
    lax.fori_loop(0, tiles, first_key, 0)
    unpack(0)
    in_do.wait()
    lax.fori_loop(0, tiles, turn_do, 0)
    after_z4()
    scores(0, 0, 1)
    after_z2()
    unpack(2)
    core_copy(0, 0).wait_recv()
    unpack(1)
    scores(1, 1, 2)
    after_y()
    unpack(4)
    core_copy(0, 1).wait_recv()
    unpack(3)
    last_scores()

    def key_terms(first, count):
        at = pl.ds(first * tok, count * tok)
        g = jnp.dot(p_t[at, :], do_v[...], preferred_element_type=f32)
        g = g + jnp.dot(ds_t[at, :], q_v[...], preferred_element_type=f32)
        gr = jnp.dot(ds_t[at, :], qr_v[...], preferred_element_type=f32)
        for k in range(count):
            b = first + k + 1 - core
            piece = slice(k * tok, (k + 1) * tok)
            turned = gr[piece, :].T
            for q in range(QUARTERS):
                gbuf[b, q, :tok, :] = g[piece, q * LANES : (q + 1) * LANES].astype(bf16)
                gbuf[b, q, tok:, :] = turned[q * 16 : (q + 1) * 16, :].astype(bf16)
        for k in range(count):
            b_copy(first + k).start()

    def a1_copy(b, k):
        return remote(
            s1.at[b, other_y(k)], ry.at[b, k - 1], a1s.at[b, k - 1], a1r.at[b, k - 1], at_y(k)
        )

    def a2_copy(n):
        return remote(sz.at[n], rz.at[n], a2s.at[n], a2r.at[n], along((-2, -4)[n // 2]))

    def a3_copy():
        return remote(sx, rx, a3s, a3r, px)

    def red1(b):
        b_arrival(b).wait_recv()
        for q in range(QUARTERS):
            s1[b, q] = (gbuf[b, q, mine].astype(f32) + rc[b, q].astype(f32)).astype(bf16)
        for k in (2, 1, 3):
            a1_copy(b, k).start()

    def red2(b):
        summed = s1[b, y].astype(f32)
        for k in (1, 2, 3):
            a1_copy(b, k).wait_recv()
            summed = summed + ry[b, k - 1].astype(f32)
        if b >= 2:
            sz[b - 2] = summed.astype(bf16)
            a2_copy(b - 2).start()
        return summed

    def f_copy(cross, k):
        block = core if cross else 1 - core
        return remote(
            fo.at[block],
            obuf.at[y, core],
            fs.at[cross, k],
            fr.at[cross, k],
            at_y(k, sib) if cross else at_y(k),
        )

    def out_copy(i):
        return pltpu.make_async_copy(dq_v.at[lanes(i)], dq_hbm.at[lanes(i)], out_sem.at[i])

    def query_terms(i, c):
        sl = lanes(i)
        turned = jnp.dot(k_t[...], ds_t[:, sl], preferred_element_type=f32)
        dq_v[sl, :] = turned[:width, :].astype(bf16).T
        qr_f[sl, :rope] = turned[width:, :].T
        out_copy(i).start()
        return c

    def query_run(first, last):
        lax.fori_loop(first, last, query_terms, 0)

    key_terms(3, 2)
    key_terms(1, 2)
    red1(5)
    red1(4)
    key_terms(0, 1)
    red1(3)
    red1(2)
    quarter = tiles // 4
    query_run(0, quarter)
    red1(1)
    red1(0)
    red2(5)
    red2(4)
    query_run(quarter, 2 * quarter)
    red2(3)
    red2(2)
    query_run(2 * quarter, 3 * quarter)
    sums = [red2(0), red2(1)]
    query_run(3 * quarter, tiles)
    for h in range(heads):
        dqr_ref[:, h * rope : (h + 1) * rope] = qr_f[pl.ds(h, tok, stride=heads), :rope].astype(bf16)

    for j in range(2):
        a2_copy(j).wait_recv()
        a2_copy(2 + j).wait_recv()
        sx[j] = (sums[j] + rz[j].astype(f32) + rz[2 + j].astype(f32)).astype(bf16)
    a3_copy().start()
    a3_copy().wait_recv()
    fo[...] = (sx[...].astype(f32) + rx[...].astype(f32)).astype(bf16)
    for k in (2, 1, 3):
        f_copy(0, k).start()
        f_copy(1, k).start()
    f_copy(1, 0).start()
    obuf[y, core] = fo[1 - core]
    for k in range(4):
        f_copy(1, k).wait_recv()
        if k:
            f_copy(0, k).wait_recv()
    for q in range(QUARTERS):
        sl = slice(q * LANES, (q + 1) * LANES)
        dlat_ref[:part, sl] = obuf[q, 0]
        dlat_ref[part:, sl] = obuf[q, 1, part - rest : tok - rest, :]
        drope_ref[q * 16 : (q + 1) * 16, :] = obuf[q, 1, tok - rest :, :]

    for i in range(tiles):
        out_copy(i).wait()
    z2_copy().wait_send()
    z4_copy().wait_send()
    for n in range(2):
        core_copy(0, n).wait_send()
    for b in range(BLOCKS):
        b_arrival(b).wait_send()
    for k in (1, 2, 3):
        y_copy(k).wait_send()
        f_copy(0, k).wait_send()
        for b in range(BLOCKS):
            a1_copy(b, k).wait_send()
    for n in range(4):
        a2_copy(n).wait_send()
        f_copy(1, n).wait_send()
    a3_copy().wait_send()


def settle(*refs):
    half = (len(refs) - 2) // 3
    sems = refs[-2:]
    copies = []
    for n in range(half):
        src, dst, room = refs[n], refs[half + n], refs[2 * half + n]
        pieces = 8 if n == 0 else 1
        step = src.shape[0] // pieces
        for p in range(pieces):
            at = pl.ds(p * step, step)
            k = len(copies)
            copies.append(
                (
                    pltpu.make_async_copy(src.at[at], room.at[at], sems[0].at[k]),
                    pltpu.make_async_copy(room.at[at], dst.at[at], sems[1].at[k]),
                )
            )
    for first, _ in copies:
        first.start()
    for first, second in copies:
        first.wait()
        second.start()
    for _, second in copies:
        second.wait()


def local(query_latent, query_rope, latent, rope_key, out_grad, doc_lengths, n_ctx):
    tok, heads, width = query_latent.shape
    rope = rope_key.shape[0]
    rows = tok * heads
    keys = SLOTS * tok
    krows = tok + rope * tok // width
    half = (krows // 2 + 15) // 16 * 16
    dma = pltpu.SemaphoreType.DMA
    vmem = pltpu.VMEM
    in_vmem = pl.BlockSpec(memory_space=pltpu.VMEM)
    in_any = pl.BlockSpec(memory_space=pl.ANY)
    shapes = (
        jax.ShapeDtypeStruct((rows, width), bf16),
        jax.ShapeDtypeStruct((tok, heads * rope), bf16),
        jax.ShapeDtypeStruct((tok, width), bf16),
        jax.ShapeDtypeStruct((rope, tok), bf16),
    )
    outs = pl.pallas_call(
        functools.partial(kernel, n_ctx, heads),
        out_shape=shapes,
        in_specs=[pl.BlockSpec(memory_space=pltpu.SMEM), in_any, in_any, in_vmem, in_vmem, in_vmem],
        out_specs=(in_any, in_vmem, in_vmem, in_vmem),
        scratch_shapes=[
            vmem((rows, width), bf16),
            vmem((rows, width), bf16),
            vmem((width + LANES, rows), bf16),
            vmem((width, rows), bf16),
            vmem((rows, LANES), f32),
            vmem((rows, LANES), bf16),
            vmem((1, rows), jnp.int32),
            vmem((8, rows), f32),
            vmem((8, rows), f32),
            vmem((keys, rows), f32),
            vmem((keys, rows), f32),
            vmem((keys, rows), bf16),
            vmem((keys, rows), bf16),
            vmem((rows, width), bf16),
            vmem((SLOTS, QUARTERS, krows, LANES), bf16),
            vmem((keys, width + LANES), bf16),
            vmem((width + rope, keys), bf16),
            vmem((BLOCKS, QUARTERS, krows, LANES), bf16),
            vmem((BLOCKS, QUARTERS, half, LANES), bf16),
            vmem((BLOCKS, QUARTERS, half, LANES), bf16),
            vmem((BLOCKS, 3, half, LANES), bf16),
            vmem((4, half, LANES), bf16),
            vmem((4, half, LANES), bf16),
            vmem((2, half, LANES), bf16),
            vmem((2, half, LANES), bf16),
            vmem((2, half, LANES), bf16),
            vmem((QUARTERS, 2, half, LANES), bf16),
            dma((2,)),
            dma((rows // TILE,)),
            dma((2,)),
            dma((2,)),
            dma((3,)),
            dma((3,)),
            dma((2,)),
            dma((2,)),
            dma((BLOCKS,)),
            dma((BLOCKS,)),
            dma((BLOCKS, 3)),
            dma((BLOCKS, 3)),
            dma((4,)),
            dma((4,)),
            dma,
            dma,
            dma((2, 4)),
            dma((2, 4)),
        ],
        compiler_params=pltpu.CompilerParams(
            collective_id=0, has_side_effects=True, vmem_limit_bytes=56 * 1024 * 1024
        ),
    )(
        doc_lengths,
        query_latent.reshape(rows, width),
        out_grad.reshape(rows, width),
        query_rope,
        latent,
        rope_key,
    )
    dq, dqr, dlat, drope = pl.pallas_call(
        settle,
        out_shape=shapes,
        in_specs=[in_any] * 4,
        out_specs=(in_any,) * 4,
        scratch_shapes=[vmem(x.shape, x.dtype) for x in shapes] + [dma((11,)), dma((11,))],
    )(*outs)
    return dq.reshape(tok, heads, width), dqr, dlat, drope


def solution(mesh):
    in_specs = (
        P("ctx", "head", None),
        P("ctx", "head"),
        P("ctx", None),
        P(None, "ctx"),
        P("ctx", "head", None),
        P(),
    )
    out_specs = (P("ctx", "head", None), P("ctx", "head"), P("ctx", None), P(None, "ctx"))
    return jax.shard_map(
        functools.partial(local, n_ctx=mesh.shape["ctx"]),
        mesh=mesh,
        in_specs=in_specs,
        out_specs=out_specs,
        check_vma=False,
    )
```

time: 70.7 us -> 54.2 us (0.77)
  the two profiles are of different devices: /device:TPU:24 before, /device:TPU:1 now
where the time goes in v2:
time: 54.2 us; the launch traced here: 54 us
  Pallas kernels  53.4 us (99%)
  between operations  0.64 us (1%)
    pallas_call x1, Pallas kernels, local(): pl.pallas_call(functools.partial(kernel, n_ctx, heads), out_shape=shapes,...  50.8 us
    pallas_call x1, Pallas kernels, local(): pl.pallas_call(settle, out_shape=shapes, in_specs=[in_any] * 4, out_specs...  2.58 us

profile of v2, /device:TPU:1, one launch (start us, length us, event | category | flops | bytes accessed | tf_op | source)
XLA Modules:
  0.0 54.0 jit_solution(227857858117736433)
XLA Ops:
  0.6 50.8 %shard_map.93 = (bf16[2048,512]{1,0:T(8,128)(2,1)}, bf16[128,1024]{1,0:T(8,128)(2,1)}, bf16[128,512]{1,0:T(8,128)(2,1)}, bf16[64,128]{1,0:T(8,128)(2,1)}) custom-call(s32[16]{0:T(128)} %len_ref.1, bf16[2048,512]{1,0:T(8,128)(2,1)} %bitcast.3, bf16[2048,512]{1,0:T(8,128)(2,1)} %bitcast.4, bf16[128,1024]{1,0:T(8,128)(2,1)} %qr_ref.1, ...), custom_call_target="tpu_custom_call" | custom-call | tf_op jit(solution)/shard_map/pallas_call | solution.py:493
  51.5 2.6 %shard_map.94 = (bf16[2048,512]{1,0:T(8,128)(2,1)}, bf16[128,1024]{1,0:T(8,128)(2,1)}, bf16[128,512]{1,0:T(8,128)(2,1)}, bf16[64,128]{1,0:T(8,128)(2,1)}) custom-call(bf16[2048,512]{1,0:T(8,128)(2,1)} %get-tuple-element.12.refs_0_, bf16[128,1024]{1,0:T(8,128)(2,1)} %get-tuple-element.13.refs_1_, bf16[128,512]{1,0:T(8,128)(2,1)} %get-tuple-element.14.refs_2_, ...), custom_call_target="tpu_custom_call" | custom-call | tf_op jit(solution)/shard_map/pallas_call | solution.py:556

commit v3 on v2

--- a/solution.py
+++ b/solution.py
@@ -14,7 +14,7 @@
 BLOCKS = SPAN + 2
 QUARTERS = 4
 LANES = 128
-TILE = 256
+TILE = 512
 softmax_scale = 192.0 ** (-0.5)
 exp2_scale = softmax_scale * math.log2(math.e)
 f32 = jnp.float32
@@ -85,7 +85,7 @@
     rope = rope_ref.shape[0]
     tiles = rows // TILE
     krows = kbuf.shape[2]
-    part = rz.shape[1]
+    part = rz.shape[2]
     rest = krows - part
 
     ctx = lax.axis_index("ctx")
@@ -145,17 +145,13 @@
     mine = pl.ds(pl.multiple_of(rest * core, 16), part)
     theirs = pl.ds(pl.multiple_of(rest * (1 - core), 16), part)
 
-    def b_copy(d):
-        b = d + 1 - core
-        return remote(gbuf.at[b, :, theirs], rc.at[b], bs.at[b], br.at[b], (sib, head))
+    def b_copy(first, count):
+        b = pl.ds(first + 1 - core, count)
+        n = (first + 1) // 2
+        return remote(gbuf.at[b, :, theirs], rc.at[b], bs.at[n], br.at[n], (sib, head))
 
     def b_unread():
-        return remote(
-            gbuf.at[unread, :, theirs], rc.at[unread], bs.at[unread], br.at[unread], (sib, head)
-        )
-
-    def b_arrival(b):
-        return remote(gbuf.at[b, :, theirs], rc.at[b], bs.at[b], br.at[b], (sib, head))
+        return remote(gbuf.at[unread, :, theirs], rc.at[unread], bs.at[3], br.at[3], (sib, head))
 
     z4_copy().start()
     z2_copy().start()
@@ -284,7 +280,7 @@
             chunk(n, first, count, i)
             return c
 
-        lax.fori_loop(0, tiles, body, 0)
+        lax.fori_loop(0, tiles, body, 0, unroll=4)
 
     def last_scores():
         def body(i, c):
@@ -292,18 +288,18 @@
             finish(i)
             return c
 
-        lax.fori_loop(0, tiles, body, 0)
+        lax.fori_loop(0, tiles, body, 0, unroll=4)
 
     in_q.wait()
-    lax.fori_loop(0, tiles, turn_q, 0)
+    lax.fori_loop(0, tiles, turn_q, 0, unroll=4)
     qr_f[...] = jnp.zeros_like(qr_f)
     for h in range(heads):
         qr_f[pl.ds(h, tok, stride=heads), :rope] = qr_ref[:, h * rope : (h + 1) * rope].astype(f32)
-    lax.fori_loop(0, tiles, turn_rope, 0)
+    lax.fori_loop(0, tiles, turn_rope, 0, unroll=4)
     lax.fori_loop(0, tiles, first_key, 0)
     unpack(0)
     in_do.wait()
-    lax.fori_loop(0, tiles, turn_do, 0)
+    lax.fori_loop(0, tiles, turn_do, 0, unroll=4)
     after_z4()
     scores(0, 0, 1)
     after_z2()
@@ -317,7 +313,7 @@
     unpack(3)
     last_scores()
 
-    def key_terms(first, count):
+    def key_dots(first, count):
         at = pl.ds(first * tok, count * tok)
         g = jnp.dot(p_t[at, :], do_v[...], preferred_element_type=f32)
         g = g + jnp.dot(ds_t[at, :], q_v[...], preferred_element_type=f32)
@@ -329,35 +325,51 @@
             for q in range(QUARTERS):
                 gbuf[b, q, :tok, :] = g[piece, q * LANES : (q + 1) * LANES].astype(bf16)
                 gbuf[b, q, tok:, :] = turned[q * 16 : (q + 1) * 16, :].astype(bf16)
-        for k in range(count):
-            b_copy(first + k).start()
-
-    def a1_copy(b, k):
+
+    def key_terms(first, count):
+        key_dots(first, count)
+        b_copy(first, count).start()
+
+    def a1_copy(pair, k):
+        two = pl.ds(2 * pair, 2)
         return remote(
-            s1.at[b, other_y(k)], ry.at[b, k - 1], a1s.at[b, k - 1], a1r.at[b, k - 1], at_y(k)
+            s1.at[other_y(k), two],
+            ry.at[k - 1, two],
+            a1s.at[pair, k - 1],
+            a1r.at[pair, k - 1],
+            at_y(k),
         )
 
-    def a2_copy(n):
-        return remote(sz.at[n], rz.at[n], a2s.at[n], a2r.at[n], along((-2, -4)[n // 2]))
+    def a2_copy(pair):
+        n = pair - 1
+        return remote(sz.at[n], rz.at[n], a2s.at[n], a2r.at[n], along(-2 * pair))
 
     def a3_copy():
         return remote(sx, rx, a3s, a3r, px)
 
-    def red1(b):
-        b_arrival(b).wait_recv()
-        for q in range(QUARTERS):
-            s1[b, q] = (gbuf[b, q, mine].astype(f32) + rc[b, q].astype(f32)).astype(bf16)
+    def red1(pair):
+        if pair == 0:
+            b_copy(0, 1).wait_recv()
+        elif pair == 1:
+            b_copy(1, 2).wait_recv()
+        else:
+            b_copy(3, 2).wait_recv()
+            b_unread().wait_recv()
+        for b in (2 * pair, 2 * pair + 1):
+            for q in range(QUARTERS):
+                s1[q, b] = (gbuf[b, q, mine].astype(f32) + rc[b, q].astype(f32)).astype(bf16)
         for k in (2, 1, 3):
-            a1_copy(b, k).start()
-
-    def red2(b):
-        summed = s1[b, y].astype(f32)
+            a1_copy(pair, k).start()
+
+    def red2(pair):
+        two = pl.ds(2 * pair, 2)
+        summed = s1[y, two].astype(f32)
         for k in (1, 2, 3):
-            a1_copy(b, k).wait_recv()
-            summed = summed + ry[b, k - 1].astype(f32)
-        if b >= 2:
-            sz[b - 2] = summed.astype(bf16)
-            a2_copy(b - 2).start()
+            a1_copy(pair, k).wait_recv()
+            summed = summed + ry[k - 1, two].astype(f32)
+        if pair:
+            sz[pair - 1] = summed.astype(bf16)
+            a2_copy(pair).start()
         return summed
 
     def f_copy(cross, k):
@@ -386,30 +398,22 @@
 
     key_terms(3, 2)
     key_terms(1, 2)
-    red1(5)
-    red1(4)
+    red1(2)
     key_terms(0, 1)
-    red1(3)
-    red1(2)
-    quarter = tiles // 4
-    query_run(0, quarter)
     red1(1)
+    query_run(0, 1)
     red1(0)
-    red2(5)
-    red2(4)
-    query_run(quarter, 2 * quarter)
-    red2(3)
+    query_run(1, tiles // 2)
     red2(2)
-    query_run(2 * quarter, 3 * quarter)
-    sums = [red2(0), red2(1)]
-    query_run(3 * quarter, tiles)
+    red2(1)
+    own = red2(0)
+    query_run(tiles // 2, tiles)
     for h in range(heads):
         dqr_ref[:, h * rope : (h + 1) * rope] = qr_f[pl.ds(h, tok, stride=heads), :rope].astype(bf16)
 
-    for j in range(2):
-        a2_copy(j).wait_recv()
-        a2_copy(2 + j).wait_recv()
-        sx[j] = (sums[j] + rz[j].astype(f32) + rz[2 + j].astype(f32)).astype(bf16)
+    a2_copy(2).wait_recv()
+    a2_copy(1).wait_recv()
+    sx[...] = (own + rz[0].astype(f32) + rz[1].astype(f32)).astype(bf16)
     a3_copy().start()
     a3_copy().wait_recv()
     fo[...] = (sx[...].astype(f32) + rx[...].astype(f32)).astype(bf16)
@@ -434,16 +438,19 @@
     z4_copy().wait_send()
     for n in range(2):
         core_copy(0, n).wait_send()
-    for b in range(BLOCKS):
-        b_arrival(b).wait_send()
+    b_copy(3, 2).wait_send()
+    b_copy(1, 2).wait_send()
+    b_copy(0, 1).wait_send()
+    b_unread().wait_send()
     for k in (1, 2, 3):
         y_copy(k).wait_send()
         f_copy(0, k).wait_send()
-        for b in range(BLOCKS):
-            a1_copy(b, k).wait_send()
+        for pair in range(3):
+            a1_copy(pair, k).wait_send()
     for n in range(4):
-        a2_copy(n).wait_send()
         f_copy(1, n).wait_send()
+    a2_copy(1).wait_send()
+    a2_copy(2).wait_send()
     a3_copy().wait_send()
 
 
@@ -515,10 +522,10 @@
             vmem((width + rope, keys), bf16),
             vmem((BLOCKS, QUARTERS, krows, LANES), bf16),
             vmem((BLOCKS, QUARTERS, half, LANES), bf16),
-            vmem((BLOCKS, QUARTERS, half, LANES), bf16),
-            vmem((BLOCKS, 3, half, LANES), bf16),
-            vmem((4, half, LANES), bf16),
-            vmem((4, half, LANES), bf16),
+            vmem((QUARTERS, BLOCKS, half, LANES), bf16),
+            vmem((3, BLOCKS, half, LANES), bf16),
+            vmem((2, 2, half, LANES), bf16),
+            vmem((2, 2, half, LANES), bf16),
             vmem((2, half, LANES), bf16),
             vmem((2, half, LANES), bf16),
             vmem((2, half, LANES), bf16),
@@ -531,12 +538,12 @@
             dma((3,)),
             dma((2,)),
             dma((2,)),
-            dma((BLOCKS,)),
-            dma((BLOCKS,)),
-            dma((BLOCKS, 3)),
-            dma((BLOCKS, 3)),
             dma((4,)),
             dma((4,)),
+            dma((3, 3)),
+            dma((3, 3)),
+            dma((2,)),
+            dma((2,)),
             dma,
             dma,
             dma((2, 4)),

time: 54.2 us -> 50.3 us (0.928)
  Pallas kernels: 53.4 us -> 49.6 us
    pallas_call x1, Pallas kernels: 50.8 us -> 47 us  [local(): pl.pallas_call(functools.partial(kernel, n_ctx, heads), out_shape=shapes,...]
where the time goes in v3:
time: 50.3 us; the launch traced here: 50.2 us
  Pallas kernels  49.6 us (99%)
  between operations  0.64 us (1%)
    pallas_call x1, Pallas kernels, local(): pl.pallas_call(functools.partial(kernel, n_ctx, heads), out_shape=shapes,...  47 us
    pallas_call x1, Pallas kernels, local(): pl.pallas_call(settle, out_shape=shapes, in_specs=[in_any] * 4, out_specs...  2.58 us

profile of v3, /device:TPU:1, one launch (start us, length us, event | category | flops | bytes accessed | tf_op | source)
XLA Modules:
  0.0 50.2 jit_solution(14610242350464924675)
XLA Ops:
  0.6 47.0 %shard_map.93 = (bf16[2048,512]{1,0:T(8,128)(2,1)}, bf16[128,1024]{1,0:T(8,128)(2,1)}, bf16[128,512]{1,0:T(8,128)(2,1)}, bf16[64,128]{1,0:T(8,128)(2,1)}) custom-call(s32[16]{0:T(128)} %len_ref.1, bf16[2048,512]{1,0:T(8,128)(2,1)} %bitcast.3, bf16[2048,512]{1,0:T(8,128)(2,1)} %bitcast.4, bf16[128,1024]{1,0:T(8,128)(2,1)} %qr_ref.1, ...), custom_call_target="tpu_custom_call" | custom-call | tf_op jit(solution)/shard_map/pallas_call | solution.py:500
  47.6 2.6 %shard_map.94 = (bf16[2048,512]{1,0:T(8,128)(2,1)}, bf16[128,1024]{1,0:T(8,128)(2,1)}, bf16[128,512]{1,0:T(8,128)(2,1)}, bf16[64,128]{1,0:T(8,128)(2,1)}) custom-call(bf16[2048,512]{1,0:T(8,128)(2,1)} %get-tuple-element.12.refs_0_, bf16[128,1024]{1,0:T(8,128)(2,1)} %get-tuple-element.13.refs_1_, bf16[128,512]{1,0:T(8,128)(2,1)} %get-tuple-element.14.refs_2_, ...), custom_call_target="tpu_custom_call" | custom-call | tf_op jit(solution)/shard_map/pallas_call | solution.py:563

commit v4 on v3

--- a/solution.py
+++ b/solution.py
@@ -27,10 +27,16 @@
     len_ref,
     q_hbm,
     do_hbm,
+    qr_hbm,
+    lat_hbm,
+    rope_hbm,
+    dq_hbm,
+    dqr_hbm,
+    dlat_hbm,
+    drope_hbm,
     qr_ref,
     lat_ref,
     rope_ref,
-    dq_hbm,
     dqr_ref,
     dlat_ref,
     drope_ref,
@@ -85,7 +91,7 @@
     rope = rope_ref.shape[0]
     tiles = rows // TILE
     krows = kbuf.shape[2]
-    part = rz.shape[2]
+    part = rz.shape[3]
     rest = krows - part
 
     ctx = lax.axis_index("ctx")
@@ -98,8 +104,8 @@
     def other_y(k):
         return (y + k) % 4
 
-    def along(by):
-        return ((ctx + by + n_ctx) % n_ctx, head)
+    def along(by, cross=0):
+        return ((ctx + by + n_ctx) % n_ctx, y * 2 + (1 - xh if cross else xh))
 
     def at_y(k, c=None):
         return (ctx if c is None else c, other_y(k) * 2 + xh)
@@ -113,21 +119,28 @@
 
     in_q = pltpu.make_async_copy(q_hbm, q_v, in_sem.at[0])
     in_do = pltpu.make_async_copy(do_hbm, do_v, in_sem.at[1])
+    in_lat = pltpu.make_async_copy(lat_hbm, lat_ref, in_sem.at[2])
+    in_rope = pltpu.make_async_copy(rope_hbm, rope_ref, in_sem.at[3])
+    in_qr = pltpu.make_async_copy(qr_hbm, qr_ref, in_sem.at[4])
+    in_lat.start()
+    in_rope.start()
 
     barrier = pltpu.get_barrier_semaphore()
-    peers = [along(by) for by in (-4, -2, 2, 4)] + [px, (sib, head)]
+    peers = [along(by, cross) for by in (-4, -2, 2, 4) for cross in (0, 1)] + [px, (sib, head)]
     for k in (1, 2, 3):
         peers += [at_y(k), at_y(k, sib)]
     for peer in peers:
         pl.semaphore_signal(barrier, inc=1, device_id=peer, device_id_type=MESH)
     in_q.start()
+    in_qr.start()
     in_do.start()
-
+    unread = (BLOCKS - 1) * core
+    gbuf[unread] = jnp.zeros(gbuf.shape[1:], bf16)
+    in_lat.wait()
+    in_rope.wait()
     for q in range(QUARTERS):
         kbuf[0, q, :tok, :] = lat_ref[:, q * LANES : (q + 1) * LANES]
         kbuf[0, q, tok:, :] = rope_ref[q * 16 : (q + 1) * 16, :]
-    unread = (BLOCKS - 1) * core
-    gbuf[unread] = jnp.zeros(gbuf.shape[1:], bf16)
     pl.semaphore_wait(barrier, len(peers))
 
     def z4_copy():
@@ -230,7 +243,7 @@
         low_v[:, lanes(i)] = low
         return c
 
-    def chunk(n, first, count, i):
+    def chunk(first, count, i):
         sl = lanes(i)
         at = pl.ds(first * tok, count * tok)
         keys = kcat[at, :]
@@ -253,38 +266,38 @@
             e = jnp.exp2((masked[k] - top) * exp2_scale)
             s_v[pl.ds((first + k) * tok, tok), sl] = e
             norm = norm + jnp.sum(e, axis=0, keepdims=True)
-        top_v[n : n + 1, sl] = top
-        norm_v[n : n + 1, sl] = norm
+        top_v[first : first + 1, sl] = top
+        norm_v[first : first + 1, sl] = norm
 
     def finish(i):
         sl = lanes(i)
-        tops = [top_v[n : n + 1, sl] for n in range(3)]
-        top = jnp.maximum(jnp.maximum(tops[0], tops[1]), tops[2])
+        tops = [top_v[d : d + 1, sl] for d in range(SLOTS)]
+        top = functools.reduce(jnp.maximum, tops)
         shares = [jnp.exp2((t - top) * exp2_scale) for t in tops]
-        norm = sum(shares[n] * norm_v[n : n + 1, sl] for n in range(3))
+        norm = sum(shares[d] * norm_v[d : d + 1, sl] for d in range(SLOTS))
         inverse = 1.0 / norm
         weights = [share * inverse for share in shares]
         delta = jnp.zeros((1, TILE), f32)
         for d in range(SLOTS):
             at = pl.ds(d * tok, tok)
-            pb = (s_v[at, sl] * weights[(d + 1) // 2]).astype(bf16)
+            pb = (s_v[at, sl] * weights[d]).astype(bf16)
             p_t[at, sl] = pb
             delta = delta + jnp.sum(pb.astype(f32) * dp_v[at, sl], axis=0, keepdims=True)
         for d in range(SLOTS):
             at = pl.ds(d * tok, tok)
-            scaled = weights[(d + 1) // 2] * softmax_scale
+            scaled = weights[d] * softmax_scale
             ds_t[at, sl] = (s_v[at, sl] * scaled * (dp_v[at, sl] - delta)).astype(bf16)
 
-    def scores(n, first, count):
+    def scores(first, count):
         def body(i, c):
-            chunk(n, first, count, i)
+            chunk(first, count, i)
             return c
 
         lax.fori_loop(0, tiles, body, 0, unroll=4)
 
-    def last_scores():
+    def last_scores(first, count):
         def body(i, c):
-            chunk(2, 3, 2, i)
+            chunk(first, count, i)
             finish(i)
             return c
 
@@ -293,6 +306,7 @@
     in_q.wait()
     lax.fori_loop(0, tiles, turn_q, 0, unroll=4)
     qr_f[...] = jnp.zeros_like(qr_f)
+    in_qr.wait()
     for h in range(heads):
         qr_f[pl.ds(h, tok, stride=heads), :rope] = qr_ref[:, h * rope : (h + 1) * rope].astype(f32)
     lax.fori_loop(0, tiles, turn_rope, 0, unroll=4)
@@ -301,17 +315,19 @@
     in_do.wait()
     lax.fori_loop(0, tiles, turn_do, 0, unroll=4)
     after_z4()
-    scores(0, 0, 1)
+    scores(0, 1)
     after_z2()
     unpack(2)
+    scores(2, 1)
     core_copy(0, 0).wait_recv()
     unpack(1)
-    scores(1, 1, 2)
+    scores(1, 1)
     after_y()
     unpack(4)
+    scores(4, 1)
     core_copy(0, 1).wait_recv()
     unpack(3)
-    last_scores()
+    last_scores(3, 1)
 
     def key_dots(first, count):
         at = pl.ds(first * tok, count * tok)
@@ -340,9 +356,15 @@
             at_y(k),
         )
 
-    def a2_copy(pair):
+    def a2_copy(pair, cross):
         n = pair - 1
-        return remote(sz.at[n], rz.at[n], a2s.at[n], a2r.at[n], along(-2 * pair))
+        return remote(
+            sz.at[n],
+            rz.at[n, cross],
+            a2s.at[n, cross],
+            a2r.at[n, cross],
+            along(-2 * pair, cross),
+        )
 
     def a3_copy():
         return remote(sx, rx, a3s, a3r, px)
@@ -369,8 +391,11 @@
             summed = summed + ry[k - 1, two].astype(f32)
         if pair:
             sz[pair - 1] = summed.astype(bf16)
-            a2_copy(pair).start()
-        return summed
+            a2_copy(pair, 1).start()
+            a2_copy(pair, 0).start()
+        else:
+            sx[...] = summed.astype(bf16)
+            a3_copy().start()
 
     def f_copy(cross, k):
         block = core if cross else 1 - core
@@ -381,6 +406,10 @@
             fr.at[cross, k],
             at_y(k, sib) if cross else at_y(k),
         )
+
+    out_dqr = pltpu.make_async_copy(dqr_ref, dqr_hbm, out_sem.at[tiles])
+    out_dlat = pltpu.make_async_copy(dlat_ref, dlat_hbm, out_sem.at[tiles + 1])
+    out_drope = pltpu.make_async_copy(drope_ref, drope_hbm, out_sem.at[tiles + 2])
 
     def out_copy(i):
         return pltpu.make_async_copy(dq_v.at[lanes(i)], dq_hbm.at[lanes(i)], out_sem.at[i])
@@ -406,22 +435,24 @@
     query_run(1, tiles // 2)
     red2(2)
     red2(1)
-    own = red2(0)
+    red2(0)
     query_run(tiles // 2, tiles)
-    for h in range(heads):
-        dqr_ref[:, h * rope : (h + 1) * rope] = qr_f[pl.ds(h, tok, stride=heads), :rope].astype(bf16)
-
-    a2_copy(2).wait_recv()
-    a2_copy(1).wait_recv()
-    sx[...] = (own + rz[0].astype(f32) + rz[1].astype(f32)).astype(bf16)
-    a3_copy().start()
+
     a3_copy().wait_recv()
-    fo[...] = (sx[...].astype(f32) + rx[...].astype(f32)).astype(bf16)
+    summed = sx[...].astype(f32) + rx[...].astype(f32)
+    for pair in (2, 1):
+        for cross in (0, 1):
+            a2_copy(pair, cross).wait_recv()
+        summed = summed + (rz[pair - 1, 0].astype(f32) + rz[pair - 1, 1].astype(f32))
+    fo[...] = summed.astype(bf16)
     for k in (2, 1, 3):
         f_copy(0, k).start()
         f_copy(1, k).start()
     f_copy(1, 0).start()
     obuf[y, core] = fo[1 - core]
+    for h in range(heads):
+        dqr_ref[:, h * rope : (h + 1) * rope] = qr_f[pl.ds(h, tok, stride=heads), :rope].astype(bf16)
+    out_dqr.start()
     for k in range(4):
         f_copy(1, k).wait_recv()
         if k:
@@ -432,6 +463,8 @@
         dlat_ref[part:, sl] = obuf[q, 1, part - rest : tok - rest, :]
         drope_ref[q * 16 : (q + 1) * 16, :] = obuf[q, 1, tok - rest :, :]
 
+    out_dlat.start()
+    out_drope.start()
     for i in range(tiles):
         out_copy(i).wait()
     z2_copy().wait_send()
@@ -449,9 +482,13 @@
             a1_copy(pair, k).wait_send()
     for n in range(4):
         f_copy(1, n).wait_send()
-    a2_copy(1).wait_send()
-    a2_copy(2).wait_send()
+    for cross in (0, 1):
+        a2_copy(1, cross).wait_send()
+        a2_copy(2, cross).wait_send()
     a3_copy().wait_send()
+    out_dqr.wait()
+    out_dlat.wait()
+    out_drope.wait()
 
 
 def settle(*refs):
@@ -489,7 +526,6 @@
     half = (krows // 2 + 15) // 16 * 16
     dma = pltpu.SemaphoreType.DMA
     vmem = pltpu.VMEM
-    in_vmem = pl.BlockSpec(memory_space=pltpu.VMEM)
     in_any = pl.BlockSpec(memory_space=pl.ANY)
     shapes = (
         jax.ShapeDtypeStruct((rows, width), bf16),
@@ -500,9 +536,15 @@
     outs = pl.pallas_call(
         functools.partial(kernel, n_ctx, heads),
         out_shape=shapes,
-        in_specs=[pl.BlockSpec(memory_space=pltpu.SMEM), in_any, in_any, in_vmem, in_vmem, in_vmem],
-        out_specs=(in_any, in_vmem, in_vmem, in_vmem),
+        in_specs=[pl.BlockSpec(memory_space=pltpu.SMEM), in_any, in_any, in_any, in_any, in_any],
+        out_specs=(in_any,) * 4,
         scratch_shapes=[
+            vmem((tok, heads * rope), bf16),
+            vmem((tok, width), bf16),
+            vmem((rope, tok), bf16),
+            vmem((tok, heads * rope), bf16),
+            vmem((tok, width), bf16),
+            vmem((rope, tok), bf16),
             vmem((rows, width), bf16),
             vmem((rows, width), bf16),
             vmem((width + LANES, rows), bf16),
@@ -525,13 +567,13 @@
             vmem((QUARTERS, BLOCKS, half, LANES), bf16),
             vmem((3, BLOCKS, half, LANES), bf16),
             vmem((2, 2, half, LANES), bf16),
-            vmem((2, 2, half, LANES), bf16),
+            vmem((2, 2, 2, half, LANES), bf16),
             vmem((2, half, LANES), bf16),
             vmem((2, half, LANES), bf16),
             vmem((2, half, LANES), bf16),
             vmem((QUARTERS, 2, half, LANES), bf16),
-            dma((2,)),
-            dma((rows // TILE,)),
+            dma((5,)),
+            dma((rows // TILE + 3,)),
             dma((2,)),
             dma((2,)),
             dma((3,)),
@@ -542,8 +584,8 @@
             dma((4,)),
             dma((3, 3)),
             dma((3, 3)),
-            dma((2,)),
-            dma((2,)),
+            dma((2, 2)),
+            dma((2, 2)),
             dma,
             dma,
             dma((2, 4)),

time: 50.3 us -> 47.3 us (0.940)
  Pallas kernels: 49.6 us -> 46.5 us
    pallas_call x1, Pallas kernels: 47 us -> 44 us  [local(): pl.pallas_call(functools.partial(kernel, n_ctx, heads), out_shape=shapes,...]
where the time goes in v4:
time: 47.3 us; the launch traced here: 47.2 us
  Pallas kernels  46.5 us (98%)
  between operations  0.64 us (1%)
    pallas_call x1, Pallas kernels, local(): pl.pallas_call(functools.partial(kernel, n_ctx, heads), out_shape=shapes,...  44 us
    pallas_call x1, Pallas kernels, local(): pl.pallas_call(settle, out_shape=shapes, in_specs=[in_any] * 4, out_specs...  2.58 us

profile of v4, /device:TPU:1, one launch (start us, length us, event | category | flops | bytes accessed | tf_op | source)
XLA Modules:
  0.0 47.2 jit_solution(6154278818977921301)
XLA Ops:
  0.6 44.0 %shard_map.93 = (bf16[2048,512]{1,0:T(8,128)(2,1)}, bf16[128,1024]{1,0:T(8,128)(2,1)}, bf16[128,512]{1,0:T(8,128)(2,1)}, bf16[64,128]{1,0:T(8,128)(2,1)}) custom-call(s32[16]{0:T(128)} %len_ref.1, bf16[2048,512]{1,0:T(8,128)(2,1)} %bitcast.3, bf16[2048,512]{1,0:T(8,128)(2,1)} %bitcast.4, bf16[128,1024]{1,0:T(8,128)(2,1)} %qr_hbm.1, ...), custom_call_target="tpu_custom_call" | custom-call | tf_op jit(solution)/shard_map/pallas_call | solution.py:536
  44.6 2.6 %shard_map.94 = (bf16[2048,512]{1,0:T(8,128)(2,1)}, bf16[128,1024]{1,0:T(8,128)(2,1)}, bf16[128,512]{1,0:T(8,128)(2,1)}, bf16[64,128]{1,0:T(8,128)(2,1)}) custom-call(bf16[2048,512]{1,0:T(8,128)(2,1)} %get-tuple-element.12.refs_0_, bf16[128,1024]{1,0:T(8,128)(2,1)} %get-tuple-element.13.refs_1_, bf16[128,512]{1,0:T(8,128)(2,1)} %get-tuple-element.14.refs_2_, ...), custom_call_target="tpu_custom_call" | custom-call | tf_op jit(solution)/shard_map/pallas_call | solution.py:605

commit v5 on v4

--- a/solution.py
+++ b/solution.py
@@ -30,16 +30,13 @@
     qr_hbm,
     lat_hbm,
     rope_hbm,
-    dq_hbm,
-    dqr_hbm,
-    dlat_hbm,
-    drope_hbm,
+    dq_v,
+    dqr_ref,
+    dlat_ref,
+    drope_ref,
     qr_ref,
     lat_ref,
     rope_ref,
-    dqr_ref,
-    dlat_ref,
-    drope_ref,
     q_v,
     do_v,
     q_t,
@@ -53,7 +50,6 @@
     dp_v,
     p_t,
     ds_t,
-    dq_v,
     kbuf,
     kcat,
     k_t,
@@ -68,7 +64,6 @@
     fo,
     obuf,
     in_sem,
-    out_sem,
     zs,
     zr,
     ys,
@@ -407,19 +402,11 @@
             at_y(k, sib) if cross else at_y(k),
         )
 
-    out_dqr = pltpu.make_async_copy(dqr_ref, dqr_hbm, out_sem.at[tiles])
-    out_dlat = pltpu.make_async_copy(dlat_ref, dlat_hbm, out_sem.at[tiles + 1])
-    out_drope = pltpu.make_async_copy(drope_ref, drope_hbm, out_sem.at[tiles + 2])
-
-    def out_copy(i):
-        return pltpu.make_async_copy(dq_v.at[lanes(i)], dq_hbm.at[lanes(i)], out_sem.at[i])
-
     def query_terms(i, c):
         sl = lanes(i)
         turned = jnp.dot(k_t[...], ds_t[:, sl], preferred_element_type=f32)
         dq_v[sl, :] = turned[:width, :].astype(bf16).T
         qr_f[sl, :rope] = turned[width:, :].T
-        out_copy(i).start()
         return c
 
     def query_run(first, last):
@@ -452,7 +439,6 @@
     obuf[y, core] = fo[1 - core]
     for h in range(heads):
         dqr_ref[:, h * rope : (h + 1) * rope] = qr_f[pl.ds(h, tok, stride=heads), :rope].astype(bf16)
-    out_dqr.start()
     for k in range(4):
         f_copy(1, k).wait_recv()
         if k:
@@ -463,10 +449,6 @@
         dlat_ref[part:, sl] = obuf[q, 1, part - rest : tok - rest, :]
         drope_ref[q * 16 : (q + 1) * 16, :] = obuf[q, 1, tok - rest :, :]
 
-    out_dlat.start()
-    out_drope.start()
-    for i in range(tiles):
-        out_copy(i).wait()
     z2_copy().wait_send()
     z4_copy().wait_send()
     for n in range(2):
@@ -486,35 +468,23 @@
         a2_copy(1, cross).wait_send()
         a2_copy(2, cross).wait_send()
     a3_copy().wait_send()
-    out_dqr.wait()
-    out_dlat.wait()
-    out_drope.wait()
 
 
 def settle(*refs):
-    half = (len(refs) - 2) // 3
-    sems = refs[-2:]
+    half = (len(refs) - 1) // 2
+    sems = refs[-1]
     copies = []
     for n in range(half):
-        src, dst, room = refs[n], refs[half + n], refs[2 * half + n]
+        src, dst = refs[n], refs[half + n]
         pieces = 8 if n == 0 else 1
         step = src.shape[0] // pieces
         for p in range(pieces):
             at = pl.ds(p * step, step)
-            k = len(copies)
-            copies.append(
-                (
-                    pltpu.make_async_copy(src.at[at], room.at[at], sems[0].at[k]),
-                    pltpu.make_async_copy(room.at[at], dst.at[at], sems[1].at[k]),
-                )
-            )
-    for first, _ in copies:
-        first.start()
-    for first, second in copies:
-        first.wait()
-        second.start()
-    for _, second in copies:
-        second.wait()
+            copies.append(pltpu.make_async_copy(src.at[at], dst.at[at], sems.at[len(copies)]))
+    for copy in copies:
+        copy.start()
+    for copy in copies:
+        copy.wait()
 
 
 def local(query_latent, query_rope, latent, rope_key, out_grad, doc_lengths, n_ctx):
@@ -535,13 +505,10 @@
     )
     outs = pl.pallas_call(
         functools.partial(kernel, n_ctx, heads),
-        out_shape=shapes,
+        out_shape=tuple(vmem(x.shape, x.dtype) for x in shapes),
         in_specs=[pl.BlockSpec(memory_space=pltpu.SMEM), in_any, in_any, in_any, in_any, in_any],
-        out_specs=(in_any,) * 4,
+        out_specs=(pl.BlockSpec(memory_space=pltpu.VMEM),) * 4,
         scratch_shapes=[
-            vmem((tok, heads * rope), bf16),
-            vmem((tok, width), bf16),
-            vmem((rope, tok), bf16),
             vmem((tok, heads * rope), bf16),
             vmem((tok, width), bf16),
             vmem((rope, tok), bf16),
@@ -558,7 +525,6 @@
             vmem((keys, rows), f32),
             vmem((keys, rows), bf16),
             vmem((keys, rows), bf16),
-            vmem((rows, width), bf16),
             vmem((SLOTS, QUARTERS, krows, LANES), bf16),
             vmem((keys, width + LANES), bf16),
             vmem((width + rope, keys), bf16),
@@ -573,7 +539,6 @@
             vmem((2, half, LANES), bf16),
             vmem((QUARTERS, 2, half, LANES), bf16),
             dma((5,)),
-            dma((rows // TILE + 3,)),
             dma((2,)),
             dma((2,)),
             dma((3,)),
@@ -607,7 +572,8 @@
         out_shape=shapes,
         in_specs=[in_any] * 4,
         out_specs=(in_any,) * 4,
-        scratch_shapes=[vmem(x.shape, x.dtype) for x in shapes] + [dma((11,)), dma((11,))],
+        scratch_shapes=[dma((11,))],
+        compiler_params=pltpu.CompilerParams(vmem_limit_bytes=1024 * 1024),
     )(*outs)
     return dq.reshape(tok, heads, width), dqr, dlat, drope
 

time: 47.3 us -> 45.5 us (0.962)
  Pallas kernels: 46.5 us -> 44.8 us
    pallas_call x1, Pallas kernels: 2.58 us -> 1.53 us  [local(): pl.pallas_call(settle, out_shape=shapes, in_specs=[in_any] * 4, out_specs...]
    pallas_call x1, Pallas kernels: 44 us -> 43.3 us  [local(): pl.pallas_call(functools.partial(kernel, n_ctx, heads), out_shape=tuple((...]
where the time goes in v5:
time: 45.5 us
  Pallas kernels  44.8 us (98%)
  between operations  0.64 us (1%)
    pallas_call x1, Pallas kernels, local(): pl.pallas_call(functools.partial(kernel, n_ctx, heads), out_shape=tuple((...  43.3 us
    pallas_call x1, Pallas kernels, local(): pl.pallas_call(settle, out_shape=shapes, in_specs=[in_any] * 4, out_specs...  1.53 us

profile of v5, /device:TPU:1, one launch (start us, length us, event | category | flops | bytes accessed | tf_op | source)
XLA Modules:
  0.0 45.5 jit_solution(1948689263947101209)
XLA Ops:
  0.6 43.3 %shard_map.93 = (bf16[2048,512]{1,0:T(8,128)(2,1)S(1)}, bf16[128,1024]{1,0:T(8,128)(2,1)S(1)}, bf16[128,512]{1,0:T(8,128)(2,1)S(1)}, bf16[64,128]{1,0:T(8,128)(2,1)S(1)}) custom-call(s32[16]{0:T(128)} %len_ref.1, bf16[2048,512]{1,0:T(8,128)(2,1)} %bitcast.3, bf16[2048,512]{1,0:T(8,128)(2,1)} %bitcast.4, bf16[128,1024]{1,0:T(8,128)(2,1)} %qr_hbm.1, ...), custom_call_target="tpu_custom_call" | custom-call | tf_op jit(solution)/shard_map/pallas_call | solution.py:506
  43.9 1.5 %shard_map.94 = (bf16[2048,512]{1,0:T(8,128)(2,1)}, bf16[128,1024]{1,0:T(8,128)(2,1)}, bf16[128,512]{1,0:T(8,128)(2,1)}, bf16[64,128]{1,0:T(8,128)(2,1)}) custom-call(bf16[2048,512]{1,0:T(8,128)(2,1)S(1)} %get-tuple-element.12.refs_0_, bf16[128,1024]{1,0:T(8,128)(2,1)S(1)} %get-tuple-element.13.refs_1_, bf16[128,512]{1,0:T(8,128)(2,1)S(1)} %get-tuple-element.14.refs_2_, ...), custom_call_target="tpu_custom_call" | custom-call | tf_op jit(solution)/shard_map/pallas_call | solution.py:570

commit v6 on v5

--- a/solution.py
+++ b/solution.py
@@ -417,13 +417,12 @@
     red1(2)
     key_terms(0, 1)
     red1(1)
+    red1(0)
     query_run(0, 1)
-    red1(0)
-    query_run(1, tiles // 2)
     red2(2)
     red2(1)
     red2(0)
-    query_run(tiles // 2, tiles)
+    query_run(1, 2)
 
     a3_copy().wait_recv()
     summed = sx[...].astype(f32) + rx[...].astype(f32)
@@ -437,6 +436,7 @@
         f_copy(1, k).start()
     f_copy(1, 0).start()
     obuf[y, core] = fo[1 - core]
+    query_run(2, tiles)
     for h in range(heads):
         dqr_ref[:, h * rope : (h + 1) * rope] = qr_f[pl.ds(h, tok, stride=heads), :rope].astype(bf16)
     for k in range(4):

time: 45.5 us -> 45.5 us (level)
  no operation moved by 1% of the time
where the time goes in v6:
time: 45.5 us; the launch traced here: 45.4 us
  Pallas kernels  44.8 us (98%)
  between operations  0.64 us (1%)
    pallas_call x1, Pallas kernels, local(): pl.pallas_call(functools.partial(kernel, n_ctx, heads), out_shape=tuple((...  43.3 us
    pallas_call x1, Pallas kernels, local(): pl.pallas_call(settle, out_shape=shapes, in_specs=[in_any] * 4, out_specs...  1.53 us

profile of v6, /device:TPU:1, one launch (start us, length us, event | category | flops | bytes accessed | tf_op | source)
XLA Modules:
  0.0 45.4 jit_solution(14939939840942339289)
XLA Ops:
  0.6 43.3 %shard_map.93 = (bf16[2048,512]{1,0:T(8,128)(2,1)S(1)}, bf16[128,1024]{1,0:T(8,128)(2,1)S(1)}, bf16[128,512]{1,0:T(8,128)(2,1)S(1)}, bf16[64,128]{1,0:T(8,128)(2,1)S(1)}) custom-call(s32[16]{0:T(128)} %len_ref.1, bf16[2048,512]{1,0:T(8,128)(2,1)} %bitcast.3, bf16[2048,512]{1,0:T(8,128)(2,1)} %bitcast.4, bf16[128,1024]{1,0:T(8,128)(2,1)} %qr_hbm.1, ...), custom_call_target="tpu_custom_call" | custom-call | tf_op jit(solution)/shard_map/pallas_call | solution.py:506
  43.9 1.5 %shard_map.94 = (bf16[2048,512]{1,0:T(8,128)(2,1)}, bf16[128,1024]{1,0:T(8,128)(2,1)}, bf16[128,512]{1,0:T(8,128)(2,1)}, bf16[64,128]{1,0:T(8,128)(2,1)}) custom-call(bf16[2048,512]{1,0:T(8,128)(2,1)S(1)} %get-tuple-element.12.refs_0_, bf16[128,1024]{1,0:T(8,128)(2,1)S(1)} %get-tuple-element.13.refs_1_, bf16[128,512]{1,0:T(8,128)(2,1)S(1)} %get-tuple-element.14.refs_2_, ...), custom_call_target="tpu_custom_call" | custom-call | tf_op jit(solution)/shard_map/pallas_call | solution.py:570
